TPU v7x, 256 devices: a whole 4x4x8 slice. The times are simulated.
256 devices in a mesh: prow: 32 (over y, x, core), pcol: 8 (over z).
Axes of the slice: x: 4, y: 4, z: 8, core: 2. Of those that a mesh axis runs over, the one named last changes fastest.
Arguments:
- right_side: bfloat16 [5, 256, 128, 256], P(None, ('prow', 'pcol')), may hold values from -6 to 6
- lower_inverse: bfloat16 [5, 256, 128, 128], P(None, ('prow', 'pcol')), may hold values from -1.5 to 1.5
- upper_inverse: bfloat16 [5, 256, 128, 128], P(None, ('prow', 'pcol')), may hold values from -1.5 to 1.5
- lower_blocks: bfloat16 [4, 256, 48, 128, 128], P(None, 'prow', 'pcol'), may hold values from -0.0546875 to 0.0546875
- lower_index: int32 [4, 256, 48], P(None, 'prow', 'pcol'), may hold values from 0 to 127, as said below
- upper_blocks: bfloat16 [4, 256, 48, 128, 128], P(None, 'prow', 'pcol'), may hold values from -0.0546875 to 0.0546875
- upper_index: int32 [4, 256, 48], P(None, 'prow', 'pcol'), may hold values from 32 to 159, as said below
Outputs:
- solution: bfloat16 [5, 256, 128, 256], P(None, ('prow', 'pcol'))
Inputs may be any that keep to these rules, and one draw needn't show every extreme that they name: lower_index[l, m, j] names a supernode of a level below l + 1; numbers may repeat. upper_index[l, m, j] names a supernode of a level above l; numbers may repeat.
All inputs are finite; a program needn't handle non-finite values.
Results may differ from a plain program's by a relative error of at most 0.014.
Values may be sent and summed in bfloat16 or wider, within the bound.
No kernel may reach another device: no remote copies, remote signals or barrier semaphores. Data moves between devices by JAX's collectives and lax.ppermute only.
A program may use at most 128 MiB of HBM per device.

v0:
```python
import jax
import jax.numpy as jnp
from jax import lax
from jax.sharding import PartitionSpec as P


def block_terms(blocks, pointers, stored):
    picked = jnp.take(stored, pointers, axis=0)
    return jnp.einsum("mkvw,mkwn->mvn", blocks, picked, preferred_element_type=jnp.float32)


def spread(solved):
    return lax.all_gather(solved, "prow", axis=0, tiled=True)


def apply_inverse(inverse, remain):
    product = jnp.einsum("uvw,uwn->uvn", inverse, remain, preferred_element_type=jnp.float32)
    return product.astype(jnp.bfloat16)


def solve_levels(
    first_inverse, inverses, blocks, pointers, sources, order, offset, per_group, levels
):
    breadth = sources[0].shape[1]
    columns = sources[0].shape[2]
    stored = jnp.zeros((levels * per_group, breadth, columns), jnp.bfloat16)
    solved = {order[0] - offset: apply_inverse(first_inverse, sources[order[0] - offset])}
    for turn in range(1, len(order)):
        height = order[turn]
        before = order[turn - 1]
        stored = lax.dynamic_update_slice_in_dim(
            stored, spread(solved[before]), before * per_group, 0
        )
        row_set = min(height, before)
        partial_value = block_terms(blocks[row_set], pointers[row_set], stored)
        totals = lax.psum_scatter(partial_value, "pcol", scatter_dimension=0, tiled=True)
        remain = (sources[height].astype(jnp.float32) - totals).astype(jnp.bfloat16)
        solved[height] = apply_inverse(inverses[height], remain)
    return solved


def shards(
    right_side, lower_inverse, upper_inverse, lower_blocks, lower_index, upper_blocks, upper_index
):
    levels = right_side.shape[0]
    per_group = lax.axis_size("prow") * right_side.shape[1]
    sources = [right_side[height] for height in range(levels)]
    forward = solve_levels(
        lower_inverse[0],
        lower_inverse,
        lower_blocks,
        lower_index,
        sources,
        list(range(levels)),
        0,
        per_group,
        levels,
    )
    lower_list = [forward[height] for height in range(levels)]
    order = list(range(levels - 1, -1, -1))
    backward = solve_levels(
        upper_inverse[levels - 1],
        upper_inverse,
        upper_blocks,
        upper_index,
        lower_list,
        order,
        0,
        per_group,
        levels,
    )
    return jnp.stack([backward[height] for height in range(levels)])


def solution(mesh):
    placed = (
        P(None, ("prow", "pcol"), None, None),
        P(None, ("prow", "pcol"), None, None),
        P(None, ("prow", "pcol"), None, None),
        P(None, "prow", "pcol", None, None),
        P(None, "prow", "pcol"),
        P(None, "prow", "pcol", None, None),
        P(None, "prow", "pcol"),
    )
    return jax.shard_map(
        shards,
        mesh=mesh,
        in_specs=placed,
        out_specs=P(None, ("prow", "pcol"), None, None),
        check_vma=False,
    )
```

profile of v0, /device:TPU:1, one launch (start us, length us, event | category | flops | bytes accessed | tf_op | source)
XLA Modules:
  0.0 869.5 jit_solution(5826913199911364753)
XLA Ops:
  9.3 53.7 %all-gather.17.cloned.1.call-done = bf16[4096,256]{1,0:T(8,128)(2,1)} async-done(((bf16[128,256]{1,0:T(8,128)(2,1)}), bf16[4096,256]{1,0:T(8,128)(2,1)}) %all-gather.17.cloned.1.call-update) | async-done | bytes 2097168 | tf_op jit(solution)/shard_map/all_gather | solution.py:13
  63.0 6.9 dynamic_update_slice.24
  69.9 4.7 gather_fusion
  82.1 32.6 %reduce-scatter.9.cloned.1.call-done = f32[1,128,256]{1,2,0:T(8,128)} async-done(((f32[8,128,256]{1,2,0:T(8,128)}), f32[1,128,256]{1,2,0:T(8,128)}) %reduce-scatter.9.cloned.1.call-update) | async-done | bytes 131088 | tf_op jit(solution)/shard_map/reduce_scatter | solution.py:36
  116.7 54.3 %all-gather.19.cloned.1.call-done = bf16[4096,256]{0,1:T(8,128)(2,1)} async-done(((bf16[128,256]{0,1:T(8,128)(2,1)}), bf16[4096,256]{0,1:T(8,128)(2,1)}) %all-gather.19.cloned.1.call-update) | async-done | bytes 2097168 | tf_op jit(solution)/shard_map/all_gather | solution.py:13
  175.8 4.7 gather_fusion.1
  187.9 32.8 %reduce-scatter.11.cloned.1.call-done = f32[1,128,256]{1,2,0:T(8,128)} async-done(((f32[8,128,256]{1,2,0:T(8,128)}), f32[1,128,256]{1,2,0:T(8,128)}) %reduce-scatter.11.cloned.1.call-update) | async-done | bytes 131088 | tf_op jit(solution)/shard_map/reduce_scatter | solution.py:36
  222.8 54.0 %all-gather.21.cloned.1.call-done = bf16[4096,256]{0,1:T(8,128)(2,1)} async-done(((bf16[128,256]{0,1:T(8,128)(2,1)}), bf16[4096,256]{0,1:T(8,128)(2,1)}) %all-gather.21.cloned.1.call-update) | async-done | bytes 2097168 | tf_op jit(solution)/shard_map/all_gather | solution.py:13
  293.8 32.8 %reduce-scatter.13.cloned.1.call-done = f32[1,128,256]{1,2,0:T(8,128)} async-done(((f32[8,128,256]{1,2,0:T(8,128)}), f32[1,128,256]{1,2,0:T(8,128)}) %reduce-scatter.13.cloned.1.call-update) | async-done | bytes 131088 | tf_op jit(solution)/shard_map/reduce_scatter | solution.py:36
  328.4 54.5 %all-gather.23.cloned.1.call-done = bf16[4096,256]{0,1:T(8,128)(2,1)} async-done(((bf16[128,256]{0,1:T(8,128)(2,1)}), bf16[4096,256]{0,1:T(8,128)(2,1)}) %all-gather.23.cloned.1.call-update) | async-done | bytes 2097168 | tf_op jit(solution)/shard_map/all_gather | solution.py:13
  387.7 4.7 gather_fusion.3
  399.9 32.8 %reduce-scatter.15.cloned.1.call-done = f32[1,128,256]{1,2,0:T(8,128)} async-done(((f32[8,128,256]{1,2,0:T(8,128)}), f32[1,128,256]{1,2,0:T(8,128)}) %reduce-scatter.15.cloned.1.call-update) | async-done | bytes 131088 | tf_op jit(solution)/shard_map/reduce_scatter | solution.py:36
  435.0 54.1 %all-gather.25.cloned.1.call-done = bf16[4096,256]{0,1:T(8,128)(2,1)} async-done(((bf16[128,256]{0,1:T(8,128)(2,1)}), bf16[4096,256]{0,1:T(8,128)(2,1)}) %all-gather.25.cloned.1.call-update) | async-done | bytes 2097168 | tf_op jit(solution)/shard_map/all_gather | solution.py:13
  492.3 5.3 dynamic_update_slice.28
  497.6 4.7 gather_fusion.4
  509.6 32.9 %reduce-scatter.17.cloned.1.call-done = f32[1,128,256]{1,2,0:T(8,128)} async-done(((f32[8,128,256]{1,2,0:T(8,128)}), f32[1,128,256]{1,2,0:T(8,128)}) %reduce-scatter.17.cloned.1.call-update) | async-done | bytes 131088 | tf_op jit(solution)/shard_map/reduce_scatter | solution.py:36
  544.6 54.3 %all-gather.27.cloned.1.call-done = bf16[4096,256]{0,1:T(8,128)(2,1)} async-done(((bf16[128,256]{0,1:T(8,128)(2,1)}), bf16[4096,256]{0,1:T(8,128)(2,1)}) %all-gather.27.cloned.1.call-update) | async-done | bytes 2097168 | tf_op jit(solution)/shard_map/all_gather | solution.py:13
  603.7 4.7 gather_fusion.5
  615.8 32.9 %reduce-scatter.19.cloned.1.call-done = f32[1,128,256]{1,2,0:T(8,128)} async-done(((f32[8,128,256]{1,2,0:T(8,128)}), f32[1,128,256]{1,2,0:T(8,128)}) %reduce-scatter.19.cloned.1.call-update) | async-done | bytes 131088 | tf_op jit(solution)/shard_map/reduce_scatter | solution.py:36
  650.8 54.2 %all-gather.29.cloned.1.call-done = bf16[4096,256]{0,1:T(8,128)(2,1)} async-done(((bf16[128,256]{0,1:T(8,128)(2,1)}), bf16[4096,256]{0,1:T(8,128)(2,1)}) %all-gather.29.cloned.1.call-update) | async-done | bytes 2097168 | tf_op jit(solution)/shard_map/all_gather | solution.py:13
  709.8 4.7 gather_fusion.6
  721.8 32.9 %reduce-scatter.21.cloned.1.call-done = f32[1,128,256]{1,2,0:T(8,128)} async-done(((f32[8,128,256]{1,2,0:T(8,128)}), f32[1,128,256]{1,2,0:T(8,128)}) %reduce-scatter.21.cloned.1.call-update) | async-done | bytes 131088 | tf_op jit(solution)/shard_map/reduce_scatter | solution.py:36
  756.6 54.4 %all-gather.31.cloned.1.call-done = bf16[4096,256]{0,1:T(8,128)(2,1)} async-done(((bf16[128,256]{0,1:T(8,128)(2,1)}), bf16[4096,256]{0,1:T(8,128)(2,1)}) %all-gather.31.cloned.1.call-update) | async-done | bytes 2097168 | tf_op jit(solution)/shard_map/all_gather | solution.py:13
  827.9 33.0 %reduce-scatter.23.cloned.1.call-done = f32[1,128,256]{2,1,0:T(8,128)} async-done(((f32[8,128,256]{2,1,0:T(8,128)}), f32[1,128,256]{2,1,0:T(8,128)}) %reduce-scatter.23.cloned.1.call-update) | async-done | bytes 131088 | tf_op jit(solution)/shard_map/reduce_scatter | solution.py:36
  (145 shorter events, 118.9 us)
Async XLA Ops:
  6.5 56.5 %all-gather.17.cloned.1.call-start = ((), (), s32[]{:S(2)}) async-start(), calls=%async_computation.16 | async-start | bytes 2162688 | tf_op jit(solution)/shard_map/all_gather | solution.py:13
  8.2 106.5 %reduce-scatter.9.cloned.1.call-start = ((), (), s32[]{:S(2)}) async-start(), calls=%async_computation.8 | async-start | bytes 1179648 | tf_op jit(solution)/shard_map/reduce_scatter | solution.py:36
  81.9 89.1 %all-gather.19.cloned.1.call-start = ((), (), s32[]{:S(2)}) async-start(), calls=%async_computation.17 | async-start | bytes 2162688 | tf_op jit(solution)/shard_map/all_gather | solution.py:13
  116.4 104.3 %reduce-scatter.11.cloned.1.call-start = ((), (), s32[]{:S(2)}) async-start(), calls=%async_computation.9 | async-start | bytes 1179648 | tf_op jit(solution)/shard_map/reduce_scatter | solution.py:36
  187.7 89.1 %all-gather.21.cloned.1.call-start = ((), (), s32[]{:S(2)}) async-start(), calls=%async_computation.18 | async-start | bytes 2162688 | tf_op jit(solution)/shard_map/all_gather | solution.py:13
  222.4 104.2 %reduce-scatter.13.cloned.1.call-start = ((), (), s32[]{:S(2)}) async-start(), calls=%async_computation.10 | async-start | bytes 1179648 | tf_op jit(solution)/shard_map/reduce_scatter | solution.py:36
  293.6 89.3 %all-gather.23.cloned.1.call-start = ((), (), s32[]{:S(2)}) async-start(), calls=%async_computation.19 | async-start | bytes 2162688 | tf_op jit(solution)/shard_map/all_gather | solution.py:13
  328.3 104.3 %reduce-scatter.15.cloned.1.call-start = ((), (), s32[]{:S(2)}) async-start(), calls=%async_computation.11 | async-start | bytes 1179648 | tf_op jit(solution)/shard_map/reduce_scatter | solution.py:36
  395.3 39.3 %copy-start.11 = (s32[4,8,6]{1,0,2:T(4,128)S(1)}, s32[4,8,6]{1,0,2:T(4,128)}, u32[]{:S(2)}) copy-start(s32[4,8,6]{1,0,2:T(4,128)} %param.15) | copy-start | bytes 2308
  399.7 89.3 %all-gather.25.cloned.1.call-start = ((), (), s32[]{:S(2)}) async-start(), calls=%async_computation.20 | async-start | bytes 2162688 | tf_op jit(solution)/shard_map/all_gather | solution.py:13
  434.5 108.1 %reduce-scatter.17.cloned.1.call-start = ((), (), s32[]{:S(2)}) async-start(), calls=%async_computation.12 | async-start | bytes 1179648 | tf_op jit(solution)/shard_map/reduce_scatter | solution.py:36
  505.1 37.4 %copy-start.7 = (bf16[256,128]{1,0:T(8,128)(2,1)S(1)}, bf16[256,128]{1,0:T(8,128)(2,1)}, u32[]{:S(2)}) copy-start(bf16[256,128]{1,0:T(8,128)(2,1)} %convolution_convert_fusion.6) | copy-start | bytes 196612
  505.1 37.4 %copy-start.10 = (bf16[5,1,128,128]{3,2,1,0:T(8,128)(2,1)S(1)}, bf16[5,1,128,128]{3,2,1,0:T(8,128)(2,1)}, u32[]{:S(2)}) copy-start(bf16[5,1,128,128]{3,2,1,0:T(8,128)(2,1)} %param.11) | copy-start | bytes 491524
  509.6 89.3 %all-gather.27.cloned.1.call-start = ((), (), s32[]{:S(2)}) async-start(), calls=%async_computation.21 | async-start | bytes 2162688 | tf_op jit(solution)/shard_map/all_gather | solution.py:13
  544.3 104.3 %reduce-scatter.19.cloned.1.call-start = ((), (), s32[]{:S(2)}) async-start(), calls=%async_computation.13 | async-start | bytes 1179648 | tf_op jit(solution)/shard_map/reduce_scatter | solution.py:36
  615.7 89.3 %all-gather.29.cloned.1.call-start = ((), (), s32[]{:S(2)}) async-start(), calls=%async_computation.22 | async-start | bytes 2162688 | tf_op jit(solution)/shard_map/all_gather | solution.py:13
  650.4 104.4 %reduce-scatter.21.cloned.1.call-start = ((), (), s32[]{:S(2)}) async-start(), calls=%async_computation.14 | async-start | bytes 1179648 | tf_op jit(solution)/shard_map/reduce_scatter | solution.py:36
  721.8 89.1 %all-gather.31.cloned.1.call-start = ((), (), s32[]{:S(2)}) async-start(), calls=%async_computation.23 | async-start | bytes 2162688 | tf_op jit(solution)/shard_map/all_gather | solution.py:13
  756.5 104.4 %reduce-scatter.23.cloned.1.call-start = ((), (), s32[]{:S(2)}) async-start(), calls=%async_computation.15 | async-start | bytes 1179648 | tf_op jit(solution)/shard_map/reduce_scatter | solution.py:36
  823.2 37.6 %copy-start.1 = (bf16[128,256]{1,0:T(8,128)(2,1)S(1)}, bf16[128,256]{1,0:T(8,128)(2,1)}, u32[]{:S(2)}) copy-start(bf16[128,256]{1,0:T(8,128)(2,1)} %convolution_convert_fusion.9) | copy-start | bytes 196612
  823.2 38.7 %copy-start.4 = (bf16[256,128]{1,0:T(8,128)(2,1)S(1)}, bf16[256,128]{1,0:T(8,128)(2,1)}, u32[]{:S(2)}) copy-start(bf16[256,128]{1,0:T(8,128)(2,1)} %convolution_convert_fusion.1) | copy-start | bytes 196612
  823.2 38.8 %copy-start.3 = (bf16[256,128]{1,0:T(8,128)(2,1)S(1)}, bf16[256,128]{1,0:T(8,128)(2,1)}, u32[]{:S(2)}) copy-start(bf16[256,128]{1,0:T(8,128)(2,1)} %convolution_convert_fusion.2) | copy-start | bytes 196612
  823.2 38.8 %copy-start.2 = (bf16[256,128]{1,0:T(8,128)(2,1)S(1)}, bf16[256,128]{1,0:T(8,128)(2,1)}, u32[]{:S(2)}) copy-start(bf16[256,128]{1,0:T(8,128)(2,1)} %convolution_convert_fusion.3) | copy-start | bytes 196612
  823.2 38.8 %copy-start = (bf16[256,128]{1,0:T(8,128)(2,1)S(1)}, bf16[256,128]{1,0:T(8,128)(2,1)}, u32[]{:S(2)}) copy-start(bf16[256,128]{1,0:T(8,128)(2,1)} %convolution_convert_fusion.4) | copy-start | bytes 196612
  (4 other events, 116.5 us)
Sparse Core Ops, SparseCore 0:
  9.9 53.0 all-gather.16
  82.1 32.6 reduce-scatter.8
  117.2 53.7 all-gather.18
  187.8 32.8 reduce-scatter.10
  223.0 53.8 all-gather.20
  293.7 32.8 reduce-scatter.12
  329.1 53.8 all-gather.22
  399.8 32.8 reduce-scatter.14
  435.1 53.8 all-gather.24
  509.7 32.8 reduce-scatter.16
  545.1 53.8 all-gather.26
  615.8 32.7 reduce-scatter.18
  651.1 53.8 all-gather.28
  721.9 32.8 reduce-scatter.20
  757.1 53.8 all-gather.30
  828.0 32.8 reduce-scatter.22
where the time goes:
time: 875 us; the launch traced here: 870 us
  waiting for transfers between devices  697 us (80%)
  local copies, waits for them, and re-layouts  108 us (12%)
  matrix products  50.2 us (6%)
  between operations  13.7 us (2%)
    all_gather x8, waiting for transfers between devices, spread(): return lax.all_gather(solved, 'prow', axis=0, tiled=True)  434 us
    reduce_scatter x8, waiting for transfers between devices, solve_levels(): lax.psum_scatter(partial_value, 'pcol', scatter_dimension=0, tiled=True)  263 us
    gather x16, local copies, waits for them, and re-layouts, block_terms(): picked = jnp.take(stored, pointers, axis=0)  60.3 us
    dot_general x8, matrix products, block_terms(): jnp.einsum('mkvw,mkwn->mvn', blocks, picked, preferred_element_type=jnp.f...  35.4 us
    all_gather x7, local copies, waits for them, and re-layouts, spread(): return lax.all_gather(solved, 'prow', axis=0, tiled=True)  22.9 us
    dynamic_update_slice x8, local copies, waits for them, and re-layouts, solve_levels(): lax.dynamic_update_slice_in_dim(stored, spread(solved[before]), before *...  21.3 us
  transfers between devices with their start and end apart: 16, of which 16 were waited for; matrix products, arithmetic and copies ran while one was open for 0% of the time, Pallas kernels for 0%

commit v1 on v0

v1 whole, which is shorter than its diff:
```python
import functools

import jax
import jax.numpy as jnp
from jax import lax
from jax.experimental import pallas as pl
from jax.experimental.pallas import tpu as pltpu
from jax.sharding import PartitionSpec as P

F32 = jnp.float32
BF16 = jnp.bfloat16


def first_kernel(own_inverse, mate_inverse, own_side, mate_side, out):
    for slot, (inverse, side) in enumerate(((own_inverse, own_side), (mate_inverse, mate_side))):
        out[slot] = jnp.dot(inverse[0], side[0], preferred_element_type=F32).astype(BF16)


def solve_kernel(terms, own_inverse, mate_inverse, own_side, mate_side, out):
    for slot, (inverse, side) in enumerate(((own_inverse, own_side), (mate_inverse, mate_side))):
        total = terms[0, slot].astype(F32)
        for source in range(1, terms.shape[0]):
            total += terms[source, slot].astype(F32)
        remain = (side[0].astype(F32) - total).astype(BF16)
        out[slot] = jnp.dot(inverse[0], remain, preferred_element_type=F32).astype(BF16)


def turn_kernel(terms, own_lower, mate_lower, own_upper, mate_upper, own_side, mate_side, low, out):
    groups = ((own_lower, own_upper, own_side), (mate_lower, mate_upper, mate_side))
    for slot, (lower, upper, side) in enumerate(groups):
        total = terms[0, slot].astype(F32)
        for source in range(1, terms.shape[0]):
            total += terms[source, slot].astype(F32)
        remain = (side[0].astype(F32) - total).astype(BF16)
        solved = jnp.dot(lower[0], remain, preferred_element_type=F32).astype(BF16)
        low[slot] = solved
        out[slot] = jnp.dot(upper[0], solved, preferred_element_type=F32).astype(BF16)


def level_spec(shape, level):
    return pl.BlockSpec((1,) + tuple(shape[1:]), lambda i: (level,) + (0,) * (len(shape) - 1))


def whole(shape):
    return pl.BlockSpec(tuple(shape), lambda i: (0,) * len(shape))


def small_call(kernel, arrays, levels, n_out):
    pair = jax.ShapeDtypeStruct((2,) + arrays[-1].shape[1:], BF16)
    specs = [
        whole(a.shape) if level is None else level_spec(a.shape, level)
        for a, level in zip(arrays, levels)
    ]
    outs = [pair] * n_out
    result = pl.pallas_call(
        kernel,
        grid=(1,),
        out_shape=outs,
        in_specs=specs,
        out_specs=[whole(pair.shape)] * n_out,
        compiler_params=pltpu.CompilerParams(vmem_limit_bytes=16 << 20),
    )(*arrays)
    return result


def rows_kernel(level, base, rows, per_row, step_rows, numbers, own, mate, stored, out):
    step = pl.program_id(0)
    for slot, blocks in enumerate((own, mate)):
        for r in range(step_rows):
            row = step * step_rows + r
            at = ((slot * (own_levels(numbers, rows, per_row)) + level) * rows + row) * per_row
            left = jnp.concatenate([blocks[0, r, k] for k in range(per_row)], axis=1)
            right = jnp.concatenate(
                [stored[numbers[at + k] - base] for k in range(per_row)], axis=0
            )
            out[r, slot] = jnp.dot(left, right, preferred_element_type=F32).astype(BF16)


def own_levels(numbers, rows, per_row):
    return numbers.shape[0] // (2 * rows * per_row)


def row_sums(level, base, numbers, own, mate, stored):
    _, rows, per_row, width, _ = own.shape
    step_rows = 2
    block = pl.BlockSpec(
        (1, step_rows, per_row, width, width), lambda i, n: (level, i, 0, 0, 0)
    )
    columns = stored.shape[2]
    return pl.pallas_call(
        functools.partial(rows_kernel, level, base, rows, per_row, step_rows),
        grid_spec=pltpu.PrefetchScalarGridSpec(
            num_scalar_prefetch=1,
            grid=(rows // step_rows,),
            in_specs=[block, block, pl.BlockSpec(memory_space=pltpu.VMEM)],
            out_specs=pl.BlockSpec((step_rows, 2, width, columns), lambda i, n: (i, 0, 0, 0)),
        ),
        out_shape=jax.ShapeDtypeStruct((rows, 2, width, columns), BF16),
        compiler_params=pltpu.CompilerParams(vmem_limit_bytes=24 << 20),
    )(numbers, own, mate, stored)


def shards(
    n_prow,
    right_side,
    lower_inverse,
    upper_inverse,
    lower_blocks,
    lower_index,
    upper_blocks,
    upper_index,
):
    levels, _, width, columns = right_side.shape
    half = columns // 2
    per_group = n_prow
    core = lax.rem(lax.axis_index("prow"), 2)
    mates = [(i, i ^ 1) for i in range(n_prow)]
    planes = [[i * 2 + c for i in range(n_prow // 2)] for c in range(2)]

    def swap(x):
        return lax.ppermute(x, "prow", mates)

    side = right_side[:, 0]
    parts = jnp.where(core == 0, side[:, :, :half], side[:, :, half:])
    others = jnp.where(core == 0, side[:, :, half:], side[:, :, :half])
    own_lower, own_upper = lower_inverse[:, 0], upper_inverse[:, 0]
    got = swap(jnp.concatenate([own_lower, own_upper, others], axis=0))
    mine = (own_lower, own_upper, parts)
    lower_mate, upper_mate = swap(lower_blocks), swap(upper_blocks)

    def numbers_of(index):
        both = jnp.stack([index, swap(index)])
        flipped = jnp.bitwise_xor(both, core)
        return flipped.reshape(-1)

    lower_numbers, upper_numbers = numbers_of(lower_index), numbers_of(upper_index)

    def spread(x):
        n = len(planes[0])
        sent = jnp.broadcast_to(x, (n,) + x.shape)
        heard = lax.all_to_all(sent, "prow", 0, 0, axis_index_groups=planes)
        return heard.reshape(per_group, width, half)

    def collect(x):
        return lax.all_to_all(x, "pcol", 0, 0)

    def source(kind, level):
        return [mine[kind], got], [level, kind * levels + level]

    def join(*groups):
        arrays, places = [], []
        for a, p in groups:
            arrays += a
            places += p
        return arrays, places

    a, p = join(source(0, 0), source(2, 0))
    (x,) = small_call(first_kernel, a, p, 1)
    low, pieces = [x], []
    for height in range(1, levels):
        pieces.append(spread(x))
        sums = row_sums(
            height - 1, 0, lower_numbers, lower_blocks, lower_mate, jnp.concatenate(pieces)
        )
        terms = ([collect(sums)], [None])
        if height < levels - 1:
            a, p = join(terms, source(0, height), source(2, height))
            (x,) = small_call(solve_kernel, a, p, 1)
            low.append(x)
        else:
            a, p = join(terms, source(0, height), source(1, height), source(2, height))
            _, x = small_call(turn_kernel, a, p, 2)
    solved, pieces = {levels - 1: x}, []
    for height in range(levels - 2, -1, -1):
        pieces.insert(0, spread(x))
        sums = row_sums(
            height,
            (height + 1) * per_group,
            upper_numbers,
            upper_blocks,
            upper_mate,
            jnp.concatenate(pieces),
        )
        terms = ([collect(sums)], [None])
        before = ([low[height], low[height]], [0, 1])
        a, p = join(terms, source(1, height), before)
        (x,) = small_call(solve_kernel, a, p, 1)
        solved[height] = x
    pairs = jnp.stack([solved[h] for h in range(levels)])
    kept, came = pairs[:, 0], swap(pairs[:, 1])
    first = jnp.where(core == 0, kept, came)
    second = jnp.where(core == 0, came, kept)
    return jnp.concatenate([first, second], axis=2)[:, None]


def solution(mesh):
    placed = (
        P(None, ("prow", "pcol"), None, None),
        P(None, ("prow", "pcol"), None, None),
        P(None, ("prow", "pcol"), None, None),
        P(None, "prow", "pcol", None, None),
        P(None, "prow", "pcol"),
        P(None, "prow", "pcol", None, None),
        P(None, "prow", "pcol"),
    )
    return jax.shard_map(
        functools.partial(shards, mesh.shape["prow"]),
        mesh=mesh,
        in_specs=placed,
        out_specs=P(None, ("prow", "pcol"), None, None),
        check_vma=False,
    )
```

time: 875 us -> 368 us (0.42)
  waiting for transfers between devices: 697 us -> 49.8 us
  blocking collectives: 0 us -> 237 us
  local copies, waits for them, and re-layouts: 108 us -> 15.8 us
  matrix products: 50.2 us -> 0 us
  Pallas kernels: 0 us -> 32.1 us
  starting transfers between devices: 0.81 us -> 27.3 us
  between operations: 13.7 us -> 0.32 us
    all_gather x8 -> x0, waiting for transfers between devices: 434 us -> none  [spread(): return lax.all_gather(solved, 'prow', axis=0, tiled=True)]
    reduce_scatter x8 -> x0, waiting for transfers between devices: 263 us -> none  [solve_levels(): lax.psum_scatter(partial_value, 'pcol', scatter_dimension=0, tiled=True)]
    all_to_all x0 -> x13, blocking collectives: none -> 237 us  [the longest x8 152 us: collect(): return lax.all_to_all(x, 'pcol', 0, 0)]
    gather x16 -> x0, local copies, waits for them, and re-layouts: 60.3 us -> none  [block_terms(): picked = jnp.take(stored, pointers, axis=0)]
    dot_general x17 -> x0, matrix products: 50.2 us -> none  [the longest x8 35.4 us: block_terms(): jnp.einsum('mkvw,mkwn->mvn', blocks, picked, preferred_element_type=jnp.f...]
    all_to_all x0 -> x3, waiting for transfers between devices: none -> 39.4 us  [spread(): heard = lax.all_to_all(sent, 'prow', 0, 0, axis_index_groups=planes)]
    pallas_call x0 -> x17, Pallas kernels: none -> 32.1 us  [the longest x8 29.6 us: row_sums(): pl.pallas_call(functools.partial(rows_kernel, level, base, rows, per_row,...]
    all_gather x7 -> x0, local copies, waits for them, and re-layouts: 22.9 us -> none  [spread(): return lax.all_gather(solved, 'prow', axis=0, tiled=True)]
  transfers between devices with their start and end apart: 16 -> 9, of which waited for: 16 -> 7; matrix products, arithmetic and copies ran while one was open for 0% -> 2% of each run, Pallas kernels for 0% -> 3%
where the time goes in v1:
time: 368 us; the launch traced here: 367 us
  blocking collectives  237 us (64%)
  waiting for transfers between devices  49.8 us (14%)
  Pallas kernels  32.1 us (9%)
  starting transfers between devices  27.3 us (7%)
  local copies, waits for them, and re-layouts  15.8 us (4%)
  other arithmetic  5.07 us (1%)
    all_to_all x8, blocking collectives, collect(): return lax.all_to_all(x, 'pcol', 0, 0)  152 us
    all_to_all x5, blocking collectives, spread(): heard = lax.all_to_all(sent, 'prow', 0, 0, axis_index_groups=planes)  85 us
    all_to_all x3, waiting for transfers between devices, spread(): heard = lax.all_to_all(sent, 'prow', 0, 0, axis_index_groups=planes)  39.4 us
    pallas_call x8, Pallas kernels, row_sums(): pl.pallas_call(functools.partial(rows_kernel, level, base, rows, per_row,...  29.6 us
    all_to_all x3, starting transfers between devices, spread(): heard = lax.all_to_all(sent, 'prow', 0, 0, axis_index_groups=planes)  15.1 us
    ppermute x6, starting transfers between devices, swap(): return lax.ppermute(x, 'prow', mates)  12.2 us
    ppermute x6, waiting for transfers between devices, swap(): return lax.ppermute(x, 'prow', mates)  10.4 us
    unnamed x24, local copies, waits for them, and re-layouts  10.4 us
  transfers between devices with their start and end apart: 9, of which 7 were waited for; matrix products, arithmetic and copies ran while one was open for 2% of the time, Pallas kernels for 3%

profile of v1, /device:TPU:1, one launch (start us, length us, event | category | flops | bytes accessed | tf_op | source)
XLA Modules:
  0.0 367.1 jit_solution(2134817196119117670)
XLA Ops:
  5.4 8.3 %collective-permute-done.4.mate_inverse.mate_side.mate_lower.mate_upper = bf16[15,128,128]{2,1,0:T(8,128)(2,1)S(1)} collective-permute-done((bf16[15,128,128]{2,1,0:T(8,128)(2,1)S(1)}, bf16[15,128,128]{2,1,0:T(8,128)(2,1)S(1)}, u32[]{:S(2)}, u32[]{:S(2)}) %collective-permute-start.4) | collective-permute-done | bytes 491552 | tf_op jit(solution)/shard_map/ppermute | solution.py:121
  16.0 5.0 %all-to-all-start = ((bf16[16,2,128,128]{3,2,1,0:T(8,128)(2,1)}), bf16[16,2,128,128]{3,2,1,0:T(8,128)(2,1)S(1)}, u32[]{:S(2)}, u32[]{:S(2)}) async-start(bf16[16,2,128,128]{3,2,1,0:T(8,128)(2,1)} %broadcast_in_dim.27), calls=%async_computation | async-start | bytes 2097152 | tf_op jit(solution)/shard_map/all_to_all | solution.py:141
  23.2 14.1 %all-to-all-done = bf16[16,2,128,128]{3,2,1,0:T(8,128)(2,1)S(1)} async-done(((bf16[16,2,128,128]{3,2,1,0:T(8,128)(2,1)}), bf16[16,2,128,128]{3,2,1,0:T(8,128)(2,1)S(1)}, u32[]{:S(2)}, u32[]{:S(2)}) %all-to-all-start) | async-done | bytes 1048608 | tf_op jit(solution)/shard_map/all_to_all | solution.py:141
  43.9 22.4 %all_to_all.80.terms = bf16[8,2,128,128]{3,2,1,0:T(8,128)(2,1)S(1)} all-to-all(bf16[8,2,128,128]{3,2,1,0:T(8,128)(2,1)S(1)} %shard_map.74), channel_id=1, replica_groups=mesh['prow'=32,'pcol'=8] {'pcol'}, dimensions={0} | all-to-all | bytes 1048576 | tf_op jit(solution)/shard_map/all_to_all | solution.py:145
  67.8 6.4 %all-to-all-start.2 = ((bf16[16,2,128,128]{3,2,1,0:T(8,128)(2,1)}), bf16[16,2,128,128]{3,2,1,0:T(8,128)(2,1)S(1)}, u32[]{:S(2)}, u32[]{:S(2)}) async-start(bf16[16,2,128,128]{3,2,1,0:T(8,128)(2,1)} %broadcast_in_dim.28), calls=%async_computation.2 | async-start | bytes 2097152 | tf_op jit(solution)/shard_map/all_to_all | solution.py:141
  76.7 12.5 %all-to-all-done.2 = bf16[16,2,128,128]{3,2,1,0:T(8,128)(2,1)S(1)} async-done(((bf16[16,2,128,128]{3,2,1,0:T(8,128)(2,1)}), bf16[16,2,128,128]{3,2,1,0:T(8,128)(2,1)S(1)}, u32[]{:S(2)}, u32[]{:S(2)}) %all-to-all-start.2) | async-done | bytes 1048608 | tf_op jit(solution)/shard_map/all_to_all | solution.py:141
  95.8 16.0 %all_to_all.81.terms = bf16[8,2,128,128]{3,2,1,0:T(8,128)(2,1)S(1)} all-to-all(bf16[8,2,128,128]{3,2,1,0:T(8,128)(2,1)S(1)} %shard_map.76), channel_id=1, replica_groups=mesh['prow'=32,'pcol'=8] {'pcol'}, dimensions={0} | all-to-all | bytes 1048576 | tf_op jit(solution)/shard_map/all_to_all | solution.py:145
  112.3 20.1 %all_to_all.82 = bf16[16,2,128,128]{3,2,1,0:T(8,128)(2,1)S(1)} all-to-all(bf16[16,2,128,128]{3,2,1,0:T(8,128)(2,1)S(1)} %broadcast_in_dim.29), channel_id=1, replica_groups={{0,16,32,48,64,80,96,112,128,144,160,176,192,208,224,240},{8,24,40,56,7..., dimensions={0} | all-to-all | bytes 2097152 | tf_op jit(solution)/shard_map/all_to_all | solution.py:141
  132.8 3.7 %shard_map.78 = bf16[8,2,128,128]{3,2,1,0:T(8,128)(2,1)S(1)} custom-call(s32[384]{0:T(512)S(1)} %xor.22.numbers, bf16[4,8,6,128,128]{4,3,2,1,0:T(8,128)(2,1)S(1)} %copy-done.1, bf16[4,8,6,128,128]{4,3,2,1,0:T(8,128)(2,1)} %collective-permute-done.3.mate, bf16[96,128,128]{2,1,0:T(8,128)(2,1)S(1)} %pad_maximum_fusion.2.stored), custom_call_target="tpu_custom_call" | custom-call | tf_op jit(solution)/shard_map/pallas_call | solution.py:90
  136.5 19.2 %all_to_all.83.terms = bf16[8,2,128,128]{3,2,1,0:T(8,128)(2,1)S(1)} all-to-all(bf16[8,2,128,128]{3,2,1,0:T(8,128)(2,1)S(1)} %shard_map.78), channel_id=1, replica_groups=mesh['prow'=32,'pcol'=8] {'pcol'}, dimensions={0} | all-to-all | bytes 1048576 | tf_op jit(solution)/shard_map/all_to_all | solution.py:145
  156.2 16.2 %all_to_all.84 = bf16[16,2,128,128]{3,2,1,0:T(8,128)(2,1)S(1)} all-to-all(bf16[16,2,128,128]{3,2,1,0:T(8,128)(2,1)S(1)} %broadcast_in_dim.30), channel_id=1, replica_groups={{0,16,32,48,64,80,96,112,128,144,160,176,192,208,224,240},{8,24,40,56,7..., dimensions={0} | all-to-all | bytes 2097152 | tf_op jit(solution)/shard_map/all_to_all | solution.py:141
  177.8 19.2 %all_to_all.85.terms = bf16[8,2,128,128]{3,2,1,0:T(8,128)(2,1)S(1)} all-to-all(bf16[8,2,128,128]{3,2,1,0:T(8,128)(2,1)S(1)} %shard_map.80), channel_id=1, replica_groups=mesh['prow'=32,'pcol'=8] {'pcol'}, dimensions={0} | all-to-all | bytes 1048576 | tf_op jit(solution)/shard_map/all_to_all | solution.py:145
  203.0 12.7 %all-to-all-done.8 = bf16[16,2,128,128]{3,2,1,0:T(8,128)(2,1)S(1)} async-done(((bf16[16,2,128,128]{3,2,1,0:T(8,128)(2,1)}), bf16[16,2,128,128]{3,2,1,0:T(8,128)(2,1)S(1)}, u32[]{:S(2)}, u32[]{:S(2)}) %all-to-all-start.8) | async-done | bytes 1048608 | tf_op jit(solution)/shard_map/all_to_all | solution.py:141
  218.5 3.7 %shard_map.82 = bf16[8,2,128,128]{3,2,1,0:T(8,128)(2,1)S(1)} custom-call(s32[384]{0:T(512)S(1)} %xor.20.numbers, bf16[4,8,6,128,128]{4,3,2,1,0:T(8,128)(2,1)S(1)} %copy-done.2, bf16[4,8,6,128,128]{4,3,2,1,0:T(8,128)(2,1)} %collective-permute-done.1.mate, bf16[32,128,128]{2,1,0:T(8,128)(2,1)S(1)} %bitcast.47), custom_call_target="tpu_custom_call" | custom-call | tf_op jit(solution)/shard_map/pallas_call | solution.py:90
  222.2 18.6 %all_to_all.86.terms = bf16[8,2,128,128]{3,2,1,0:T(8,128)(2,1)S(1)} all-to-all(bf16[8,2,128,128]{3,2,1,0:T(8,128)(2,1)S(1)} %shard_map.82), channel_id=1, replica_groups=mesh['prow'=32,'pcol'=8] {'pcol'}, dimensions={0} | all-to-all | bytes 1048576 | tf_op jit(solution)/shard_map/all_to_all | solution.py:145
  241.2 17.9 %all_to_all.87 = bf16[16,2,128,128]{3,2,1,0:T(8,128)(2,1)S(1)} all-to-all(bf16[16,2,128,128]{3,2,1,0:T(8,128)(2,1)S(1)} %broadcast_in_dim.32), channel_id=1, replica_groups={{0,16,32,48,64,80,96,112,128,144,160,176,192,208,224,240},{8,24,40,56,7..., dimensions={0} | all-to-all | bytes 2097152 | tf_op jit(solution)/shard_map/all_to_all | solution.py:141
  259.3 3.7 %shard_map.84 = bf16[8,2,128,128]{3,2,1,0:T(8,128)(2,1)S(1)} custom-call(s32[384]{0:T(512)S(1)} %xor.20.numbers, bf16[4,8,6,128,128]{4,3,2,1,0:T(8,128)(2,1)S(1)} %copy-done.2, bf16[4,8,6,128,128]{4,3,2,1,0:T(8,128)(2,1)} %collective-permute-done.1.mate, bf16[64,128,128]{2,1,0:T(8,128)(2,1)S(1)} %pad_maximum_fusion.5.stored), custom_call_target="tpu_custom_call" | custom-call | tf_op jit(solution)/shard_map/pallas_call | solution.py:90
  263.0 19.1 %all_to_all.88.terms = bf16[8,2,128,128]{3,2,1,0:T(8,128)(2,1)S(1)} all-to-all(bf16[8,2,128,128]{3,2,1,0:T(8,128)(2,1)S(1)} %shard_map.84), channel_id=1, replica_groups=mesh['prow'=32,'pcol'=8] {'pcol'}, dimensions={0} | all-to-all | bytes 1048576 | tf_op jit(solution)/shard_map/all_to_all | solution.py:145
  282.6 15.0 %all_to_all.89 = bf16[16,2,128,128]{3,2,1,0:T(8,128)(2,1)S(1)} all-to-all(bf16[16,2,128,128]{3,2,1,0:T(8,128)(2,1)S(1)} %broadcast_in_dim.33), channel_id=1, replica_groups={{0,16,32,48,64,80,96,112,128,144,160,176,192,208,224,240},{8,24,40,56,7..., dimensions={0} | all-to-all | bytes 2097152 | tf_op jit(solution)/shard_map/all_to_all | solution.py:141
  298.0 3.7 %shard_map.86 = bf16[8,2,128,128]{3,2,1,0:T(8,128)(2,1)S(1)} custom-call(s32[384]{0:T(512)S(1)} %xor.20.numbers, bf16[4,8,6,128,128]{4,3,2,1,0:T(8,128)(2,1)S(1)} %copy-done.2, bf16[4,8,6,128,128]{4,3,2,1,0:T(8,128)(2,1)} %collective-permute-done.1.mate, bf16[96,128,128]{2,1,0:T(8,128)(2,1)S(1)} %pad_maximum_fusion.3.stored), custom_call_target="tpu_custom_call" | custom-call | tf_op jit(solution)/shard_map/pallas_call | solution.py:90
  301.7 19.4 %all_to_all.90.terms = bf16[8,2,128,128]{3,2,1,0:T(8,128)(2,1)S(1)} all-to-all(bf16[8,2,128,128]{3,2,1,0:T(8,128)(2,1)S(1)} %shard_map.86), channel_id=1, replica_groups=mesh['prow'=32,'pcol'=8] {'pcol'}, dimensions={0} | all-to-all | bytes 1048576 | tf_op jit(solution)/shard_map/all_to_all | solution.py:145
  321.5 15.8 %all_to_all.91 = bf16[16,2,128,128]{3,2,1,0:T(8,128)(2,1)S(1)} all-to-all(bf16[16,2,128,128]{3,2,1,0:T(8,128)(2,1)S(1)} %broadcast_in_dim.34), channel_id=1, replica_groups={{0,16,32,48,64,80,96,112,128,144,160,176,192,208,224,240},{8,24,40,56,7..., dimensions={0} | all-to-all | bytes 2097152 | tf_op jit(solution)/shard_map/all_to_all | solution.py:141
  341.5 17.9 %all_to_all.92.terms = bf16[8,2,128,128]{3,2,1,0:T(8,128)(2,1)S(1)} all-to-all(bf16[8,2,128,128]{3,2,1,0:T(8,128)(2,1)S(1)} %shard_map.88), channel_id=1, replica_groups=mesh['prow'=32,'pcol'=8] {'pcol'}, dimensions={0} | all-to-all | bytes 1048576 | tf_op jit(solution)/shard_map/all_to_all | solution.py:145
  359.7 5.5 %collective-permute-start.5 = (bf16[5,128,128]{2,1,0:T(8,128)(2,1)S(1)}, bf16[5,128,128]{2,1,0:T(8,128)(2,1)S(1)}, u32[]{:S(2)}, u32[]{:S(2)}) collective-permute-start(bf16[5,128,128]{2,1,0:T(8,128)(2,1)S(1)} %slice_bitcast_fusion), channel_id=1, source_target_pairs={{0,8},{8,0},{16,24},{24,16},{32,40},{40,32},{48,56},{56,48},{64,72... | collective-permute-start | bytes 491528 | tf_op jit(solution)/shard_map/ppermute | solution.py:121
  (74 shorter events, 50.6 us)
Async XLA Ops:
  0.0 21.0 %copy-start.7 = (s32[4,8,6]{1,0,2:T(4,128)S(1)}, s32[4,8,6]{1,0,2:T(4,128)}, u32[]{:S(2)}) copy-start(s32[4,8,6]{1,0,2:T(4,128)} %param.11) | copy-start | bytes 2308
  0.0 21.8 %copy-start.6 = (s32[4,8,6]{1,0,2:T(4,128)S(1)}, s32[4,8,6]{1,0,2:T(4,128)}, u32[]{:S(2)}) copy-start(s32[4,8,6]{1,0,2:T(4,128)} %param.13) | copy-start | bytes 2308
  0.0 37.4 %collective-permute-start.3 = (bf16[4,8,6,128,128]{4,3,2,1,0:T(8,128)(2,1)}, bf16[4,8,6,128,128]{4,3,2,1,0:T(8,128)(2,1)}, u32[]{:S(2)}, u32[]{:S(2)}) collective-permute-start(bf16[4,8,6,128,128]{4,3,2,1,0:T(8,128)(2,1)} %own.11), channel_id=1, source_target_pairs={{0,8},{8,0},{16,24},{24,16},{32,40},{40,32},{48,56},{56,48},{64,72... | collective-permute-start | bytes 18874376 | tf_op jit(solution)/shard_map/ppermute | solution.py:121
  5.3 8.4 %collective-permute-start.4 = (bf16[15,128,128]{2,1,0:T(8,128)(2,1)S(1)}, bf16[15,128,128]{2,1,0:T(8,128)(2,1)S(1)}, u32[]{:S(2)}, u32[]{:S(2)}) collective-permute-start(bf16[15,128,128]{2,1,0:T(8,128)(2,1)S(1)} %pad_maximum_fusion.6), channel_id=1, source_target_pairs={{0,8},{8,0},{16,24},{24,16},{32,40},{40,32},{48,56},{56,48},{64,72... | collective-permute-start | bytes 1474568 | tf_op jit(solution)/shard_map/ppermute | solution.py:121
  13.7 0.9 copy-start.3
  16.0 21.4 %all-to-all-start = ((bf16[16,2,128,128]{3,2,1,0:T(8,128)(2,1)}), bf16[16,2,128,128]{3,2,1,0:T(8,128)(2,1)S(1)}, u32[]{:S(2)}, u32[]{:S(2)}) async-start(bf16[16,2,128,128]{3,2,1,0:T(8,128)(2,1)} %broadcast_in_dim.27), calls=%async_computation | async-start | bytes 2097152 | tf_op jit(solution)/shard_map/all_to_all | solution.py:141
  21.1 1.6 collective-permute-start.2
  21.8 1.2 collective-permute-start
  37.4 2.8 copy-start
  40.2 26.1 %copy-start.4 = (bf16[5,1,128,128]{3,2,1,0:T(8,128)(2,1)S(1)}, bf16[5,1,128,128]{3,2,1,0:T(8,128)(2,1)}, u32[]{:S(2)}) copy-start(bf16[5,1,128,128]{3,2,1,0:T(8,128)(2,1)} %param.8) | copy-start | bytes 491524
  67.8 21.4 %all-to-all-start.2 = ((bf16[16,2,128,128]{3,2,1,0:T(8,128)(2,1)}), bf16[16,2,128,128]{3,2,1,0:T(8,128)(2,1)S(1)}, u32[]{:S(2)}, u32[]{:S(2)}) async-start(bf16[16,2,128,128]{3,2,1,0:T(8,128)(2,1)} %broadcast_in_dim.28), calls=%async_computation.2 | async-start | bytes 2097152 | tf_op jit(solution)/shard_map/all_to_all | solution.py:141
  74.2 128.8 %collective-permute-start.1 = (bf16[4,8,6,128,128]{4,3,2,1,0:T(8,128)(2,1)}, bf16[4,8,6,128,128]{4,3,2,1,0:T(8,128)(2,1)}, u32[]{:S(2)}, u32[]{:S(2)}) collective-permute-start(bf16[4,8,6,128,128]{4,3,2,1,0:T(8,128)(2,1)} %own.15), channel_id=1, source_target_pairs={{0,8},{8,0},{16,24},{24,16},{32,40},{40,32},{48,56},{56,48},{64,72... | collective-permute-start | bytes 18874376 | tf_op jit(solution)/shard_map/ppermute | solution.py:121
  89.4 2.8 copy-start.1
  156.0 17.0 %slice-start = ((s8[6291456]{0:T(1024)(128)(4,1)}), s8[4194304]{0:T(1024)(128)(4,1)S(1)}, s32[]{:S(2)}) async-start(s8[6291456]{0:T(1024)(128)(4,1)} %bitcast.41), calls=%async_computation.16 | async-start | bytes 8388608
  172.4 1.6 slice-start.1
  174.0 22.9 %copy-start.5 = (bf16[5,1,128,128]{3,2,1,0:T(8,128)(2,1)S(1)}, bf16[5,1,128,128]{3,2,1,0:T(8,128)(2,1)}, u32[]{:S(2)}) copy-start(bf16[5,1,128,128]{3,2,1,0:T(8,128)(2,1)} %param.9) | copy-start | bytes 491524
  199.0 16.6 %all-to-all-start.8 = ((bf16[16,2,128,128]{3,2,1,0:T(8,128)(2,1)}), bf16[16,2,128,128]{3,2,1,0:T(8,128)(2,1)S(1)}, u32[]{:S(2)}, u32[]{:S(2)}) async-start(bf16[16,2,128,128]{3,2,1,0:T(8,128)(2,1)} %broadcast_in_dim.31), calls=%async_computation.8 | async-start | bytes 2097152 | tf_op jit(solution)/shard_map/all_to_all | solution.py:141
  215.7 2.8 copy-start.2
  359.7 6.6 %collective-permute-start.5 = (bf16[5,128,128]{2,1,0:T(8,128)(2,1)S(1)}, bf16[5,128,128]{2,1,0:T(8,128)(2,1)S(1)}, u32[]{:S(2)}, u32[]{:S(2)}) collective-permute-start(bf16[5,128,128]{2,1,0:T(8,128)(2,1)S(1)} %slice_bitcast_fusion), channel_id=1, source_target_pairs={{0,8},{8,0},{16,24},{24,16},{32,40},{40,32},{48,56},{56,48},{64,72... | collective-permute-start | bytes 491528 | tf_op jit(solution)/shard_map/ppermute | solution.py:121

commit v2 on v0

v2 whole, which is shorter than its diff:
```python
import functools

import jax
import jax.numpy as jnp
from jax import lax
from jax.experimental import pallas as pl
from jax.experimental.pallas import tpu as pltpu
from jax.sharding import PartitionSpec as P

F32 = jnp.float32
BF16 = jnp.bfloat16


def first_kernel(core, side, lower, upper, kept, mine, given):
    levels, _, width, columns = side.shape
    half = columns // 2
    here = pl.ds(pl.multiple_of(core[0] * half, half), half)
    there = pl.ds(pl.multiple_of((1 - core[0]) * half, half), half)
    for out, part in ((mine, here), (given, there)):
        for level in range(levels):
            out[level] = lower[level, 0]
            out[levels + level] = upper[level, 0]
            out[2 * levels + level] = side[level, 0, :, part]
    inverse = lower[0, 0]
    kept[...] = jnp.dot(inverse, side[0, 0, :, here], preferred_element_type=F32).astype(BF16)
    given[3 * levels] = jnp.dot(
        inverse, side[0, 0, :, there], preferred_element_type=F32
    ).astype(BF16)


def first_call(core, side, lower, upper):
    levels, _, width, columns = side.shape
    half = columns // 2
    vmem = pl.BlockSpec(memory_space=pltpu.VMEM)
    return pl.pallas_call(
        first_kernel,
        grid_spec=pltpu.PrefetchScalarGridSpec(
            num_scalar_prefetch=1,
            grid=(1,),
            in_specs=[
                pl.BlockSpec(x.shape, lambda i, c: (0, 0, 0, 0)) for x in (side, lower, upper)
            ],
            out_specs=[vmem] * 3,
        ),
        out_shape=[
            jax.ShapeDtypeStruct((width, half), BF16),
            jax.ShapeDtypeStruct((3 * levels, width, half), BF16),
            jax.ShapeDtypeStruct((3 * levels + 1, width, half), BF16),
        ],
        compiler_params=pltpu.CompilerParams(vmem_limit_bytes=16 << 20),
    )(core, side, lower, upper)


def spread_kernel(kept, got, *rest):
    out = rest[-1]
    last = got.shape[0] - 1
    for i in range(out.shape[0]):
        out[i, 0] = kept[...]
        out[i, 1] = got[last]


def spread_call(copies, kept, got, others):
    shape = (copies, 2) + kept.shape
    return pl.pallas_call(
        spread_kernel,
        in_specs=[pl.BlockSpec(memory_space=pltpu.VMEM)] * 2
        + [pl.BlockSpec(memory_space=pl.ANY)] * len(others),
        out_specs=pl.BlockSpec(memory_space=pltpu.VMEM),
        out_shape=jax.ShapeDtypeStruct(shape, BF16),
        compiler_params=pltpu.CompilerParams(vmem_limit_bytes=16 << 20),
    )(kept, got, *others)


def remain_of(terms, slot, side):
    total = terms[0, slot].astype(F32)
    for source in range(1, terms.shape[0]):
        total += terms[source, slot].astype(F32)
    return (side.astype(F32) - total).astype(BF16)


def solve_kernel(picks, terms, mine, got, *refs):
    side_pick, inverse_picks, n_before = picks
    before, outs = refs[:n_before], refs[n_before:]
    for slot, packed in enumerate((mine, got)):
        if side_pick is not None:
            side = packed[side_pick]
        elif len(before) == 1:
            side = before[0][slot]
        else:
            kept, came = before
            side = came[came.shape[0] - 1] if slot else kept[...]
        x = remain_of(terms, slot, side)
        for pick in inverse_picks:
            x = jnp.dot(packed[pick], x, preferred_element_type=F32).astype(BF16)
        outs[0][slot] = x
        for sent in outs[1:]:
            for i in range(sent.shape[0]):
                sent[i, slot] = x


def solve_call(side_pick, inverse_picks, copies, terms, mine, got, before=()):
    _, pair, width, half = terms.shape
    outs = [jax.ShapeDtypeStruct((pair, width, half), BF16)]
    if copies:
        outs.append(jax.ShapeDtypeStruct((copies, pair, width, half), BF16))
    vmem = pl.BlockSpec(memory_space=pltpu.VMEM)
    return pl.pallas_call(
        functools.partial(solve_kernel, (side_pick, inverse_picks, len(before))),
        in_specs=[vmem] * (3 + len(before)),
        out_specs=[vmem] * len(outs),
        out_shape=outs,
        compiler_params=pltpu.CompilerParams(vmem_limit_bytes=16 << 20),
    )(terms, mine, got, *before)


def rows_kernel(level, base, which, fetch, numbers, own, mate, stored, *rest):
    levels, rows, per_row = own.shape[:3]
    out = rest[-3] if fetch else rest[-1]
    if fetch:
        held, sems = rest[-2:]
        cut = rows // sems.shape[0]

        def copy(i):
            part = pl.ds(i * cut, cut)
            return pltpu.make_async_copy(own.at[level, part], held.at[part], sems.at[i])

        for i in range(sems.shape[0]):
            copy(i).start()
    for slot in (1, 0):
        if fetch and slot == 0:
            for i in range(sems.shape[0]):
                copy(i).wait()
        for row in range(rows):
            at = (((slot * 2 + which) * levels + level) * rows + row) * per_row
            if slot:
                blocks = [mate[level, row, k] for k in range(per_row)]
            elif fetch:
                blocks = [held[row, k] for k in range(per_row)]
            else:
                blocks = [own[level, row, k] for k in range(per_row)]
            left = jnp.concatenate(blocks, axis=1)
            right = jnp.concatenate(
                [stored[numbers[at + k] - base] for k in range(per_row)], axis=0
            )
            out[row, slot] = jnp.dot(left, right, preferred_element_type=F32).astype(BF16)


def row_sums(level, base, which, numbers, own, mate, stored, others=(), fetch=False):
    _, rows, per_row, width, _ = own.shape
    columns = stored.shape[2]
    vmem = pl.BlockSpec(memory_space=pltpu.VMEM)
    first, scratch = vmem, []
    if fetch:
        own = pltpu.with_memory_space_constraint(own, pltpu.HBM)
        first = pl.BlockSpec(memory_space=pltpu.HBM)
        scratch = [
            pltpu.VMEM((rows, per_row, width, width), BF16),
            pltpu.SemaphoreType.DMA((2,)),
        ]
    return pl.pallas_call(
        functools.partial(rows_kernel, level, base, which, fetch),
        grid_spec=pltpu.PrefetchScalarGridSpec(
            num_scalar_prefetch=1,
            grid=(1,),
            in_specs=[first, vmem, vmem] + [vmem] * len(others),
            out_specs=vmem,
            scratch_shapes=scratch,
        ),
        out_shape=jax.ShapeDtypeStruct((rows, 2, width, columns), BF16),
        compiler_params=pltpu.CompilerParams(vmem_limit_bytes=8 << 20),
    )(numbers, own, mate, stored, *others)


def shards(
    n_prow,
    right_side,
    lower_inverse,
    upper_inverse,
    lower_blocks,
    lower_index,
    upper_blocks,
    upper_index,
):
    levels, _, width, columns = right_side.shape
    half = columns // 2
    core = lax.rem(lax.axis_index("prow"), 2).astype(jnp.int32)
    core_ref = core.reshape(1)
    mates = [(i, i ^ 1) for i in range(n_prow)]
    planes = [[i * 2 + c for i in range(n_prow // 2)] for c in range(2)]
    copies = n_prow // 2

    def swap(x):
        return lax.ppermute(x, "prow", mates)

    small = [right_side, lower_inverse, upper_inverse]
    small = [pltpu.with_memory_space_constraint(x, pltpu.HBM) for x in small]
    kept, mine, given = first_call(core_ref, *small)
    got = swap(given)
    index = jnp.stack([lower_index, upper_index]).reshape(-1)
    index = lax.optimization_barrier(index)
    numbers = jnp.bitwise_xor(jnp.concatenate([index, swap(index)]), core)
    lower_given, upper_given, _, _ = lax.optimization_barrier(
        (lower_blocks, upper_blocks, got, numbers)
    )
    lower_mate, upper_mate = swap(lower_given), swap(upper_given)

    def heard(sent):
        got = lax.all_to_all(sent, "prow", 0, 0, axis_index_groups=planes)
        return got.reshape(n_prow, width, half)

    def collect(x):
        return lax.all_to_all(x, "pcol", 0, 0)

    sent = spread_call(copies, kept, got, [numbers])
    low, pieces = [(kept, got)], [heard(sent)]
    for height in range(1, levels):
        sums = row_sums(
            height - 1,
            0,
            0,
            numbers,
            lower_blocks,
            lower_mate,
            jnp.concatenate(pieces),
            [upper_mate] if height == 2 else [],
            height == 1,
        )
        turn = height == levels - 1
        picks = [height, levels + height] if turn else [height]
        x, sent = solve_call(2 * levels + height, picks, copies, collect(sums), mine, got)
        if not turn:
            low.append((x,))
            pieces.append(heard(sent))
    solved, pieces = {levels - 1: x}, []
    for height in range(levels - 2, -1, -1):
        pieces.insert(0, heard(sent))
        sums = row_sums(
            height,
            (height + 1) * n_prow,
            1,
            numbers,
            upper_blocks,
            upper_mate,
            jnp.concatenate(pieces),
        )
        x, *sent = solve_call(
            None,
            [levels + height],
            copies if height else 0,
            collect(sums),
            mine,
            got,
            low[height],
        )
        sent = sent[0] if sent else None
        solved[height] = x
    pairs = jnp.stack([solved[h] for h in range(levels)])
    kept, came = pairs[:, 0], swap(pairs[:, 1])
    first = jnp.where(core == 0, kept, came)
    second = jnp.where(core == 0, came, kept)
    return jnp.concatenate([first, second], axis=2)[:, None]


def solution(mesh):
    placed = (
        P(None, ("prow", "pcol"), None, None),
        P(None, ("prow", "pcol"), None, None),
        P(None, ("prow", "pcol"), None, None),
        P(None, "prow", "pcol", None, None),
        P(None, "prow", "pcol"),
        P(None, "prow", "pcol", None, None),
        P(None, "prow", "pcol"),
    )
    return jax.shard_map(
        functools.partial(shards, mesh.shape["prow"]),
        mesh=mesh,
        in_specs=placed,
        out_specs=P(None, ("prow", "pcol"), None, None),
        check_vma=False,
    )
```

time: 875 us -> 322 us (0.37)
  waiting for transfers between devices: 697 us -> 2.18 us
  blocking collectives: 0 us -> 286 us
  local copies, waits for them, and re-layouts: 108 us -> 0.36 us
  matrix products: 50.2 us -> 0 us
  Pallas kernels: 0 us -> 18.3 us
  between operations: 13.7 us -> 0.25 us
  starting transfers between devices: 0.81 us -> 10.2 us
    all_gather x8 -> x0, waiting for transfers between devices: 434 us -> none  [spread(): return lax.all_gather(solved, 'prow', axis=0, tiled=True)]
    all_to_all x0 -> x16, blocking collectives: none -> 286 us  [the longest x8 154 us: collect(): return lax.all_to_all(x, 'pcol', 0, 0)]
    reduce_scatter x8 -> x0, waiting for transfers between devices: 263 us -> none  [solve_levels(): lax.psum_scatter(partial_value, 'pcol', scatter_dimension=0, tiled=True)]
    gather x16 -> x0, local copies, waits for them, and re-layouts: 60.3 us -> none  [block_terms(): picked = jnp.take(stored, pointers, axis=0)]
    dot_general x17 -> x0, matrix products: 50.2 us -> none  [the longest x8 35.4 us: block_terms(): jnp.einsum('mkvw,mkwn->mvn', blocks, picked, preferred_element_type=jnp.f...]
    all_gather x7 -> x0, local copies, waits for them, and re-layouts: 22.9 us -> none  [spread(): return lax.all_gather(solved, 'prow', axis=0, tiled=True)]
    dynamic_update_slice x8 -> x0, local copies, waits for them, and re-layouts: 21.3 us -> none  [solve_levels(): lax.dynamic_update_slice_in_dim(stored, spread(solved[before]), before *...]
    pallas_call x0 -> x18, Pallas kernels: none -> 18.3 us  [the longest x8 14.4 us: row_sums(): pl.pallas_call(functools.partial(rows_kernel, level, base, which, fetch),...]
  transfers between devices with their start and end apart: 16 -> 5, of which waited for: 16 -> 2; matrix products, arithmetic and copies ran while one was open for 0% -> 0% of each run, Pallas kernels for 0% -> 1%
where the time goes in v2:
time: 322 us; the launch traced here: 321 us
  blocking collectives  286 us (89%)
  Pallas kernels  18.3 us (6%)
  starting transfers between devices  10.2 us (3%)
  other arithmetic  3.72 us (1%)
    all_to_all x8, blocking collectives, collect(): return lax.all_to_all(x, 'pcol', 0, 0)  154 us
    all_to_all x8, blocking collectives, heard(): got = lax.all_to_all(sent, 'prow', 0, 0, axis_index_groups=planes)  132 us
    pallas_call x8, Pallas kernels, row_sums(): pl.pallas_call(functools.partial(rows_kernel, level, base, which, fetch),...  14.4 us
    ppermute x5, starting transfers between devices, swap(): return lax.ppermute(x, 'prow', mates)  10.2 us
  transfers between devices with their start and end apart: 5, of which 2 were waited for; matrix products, arithmetic and copies ran while one was open for 0% of the time, Pallas kernels for 1%

profile of v2, /device:TPU:1, one launch (start us, length us, event | category | flops | bytes accessed | tf_op | source)
XLA Modules:
  0.0 320.8 jit_solution(17497326295376337145)
XLA Ops:
  1.4 3.3 %collective-permute-start.1 = (bf16[16,128,128]{2,1,0:T(8,128)(2,1)S(1)}, bf16[16,128,128]{2,1,0:T(8,128)(2,1)S(1)}, u32[]{:S(2)}, u32[]{:S(2)}) collective-permute-start(bf16[16,128,128]{2,1,0:T(8,128)(2,1)S(1)} %get-tuple-element.24), channel_id=1, source_target_pairs={{0,8},{8,0},{16,24},{24,16},{32,40},{40,32},{48,56},{56,48},{64,72... | collective-permute-start | bytes 1572872 | tf_op jit(solution)/shard_map/ppermute | solution.py:193
  7.7 21.3 %all_to_all.80 = bf16[16,2,128,128]{3,2,1,0:T(8,128)(2,1)S(1)} all-to-all(bf16[16,2,128,128]{3,2,1,0:T(8,128)(2,1)S(1)} %shard_map.74), channel_id=1, replica_groups={{0,16,32,48,64,80,96,112,128,144,160,176,192,208,224,240},{8,24,40,56,7..., dimensions={0} | all-to-all | bytes 2097152 | tf_op jit(solution)/shard_map/all_to_all | solution.py:208
  29.0 3.4 %shard_map.75 = bf16[8,2,128,128]{3,2,1,0:T(8,128)(2,1)S(1)} custom-call(s32[768]{0:T(1024)S(1)} %add_xor_fusion.rest_0_.numbers, bf16[4,8,6,128,128]{4,3,2,1,0:T(8,128)(2,1)} %own.11, bf16[4,8,6,128,128]{4,3,2,1,0:T(8,128)(2,1)S(1)} %collective-permute-done.3.mate, bf16[32,128,128]{2,1,0:T(8,128)(2,1)S(1)} %bitcast.41), custom_call_target="tpu_custom_call" | custom-call | tf_op jit(solution)/shard_map/pallas_call | solution.py:160
  32.5 22.7 %all_to_all.81.terms = bf16[8,2,128,128]{3,2,1,0:T(8,128)(2,1)S(1)} all-to-all(bf16[8,2,128,128]{3,2,1,0:T(8,128)(2,1)S(1)} %shard_map.75), channel_id=1, replica_groups=mesh['prow'=32,'pcol'=8] {'pcol'}, dimensions={0} | all-to-all | bytes 1048576 | tf_op jit(solution)/shard_map/all_to_all | solution.py:212
  55.4 18.1 %all_to_all.82 = bf16[16,2,128,128]{3,2,1,0:T(8,128)(2,1)S(1)} all-to-all(bf16[16,2,128,128]{3,2,1,0:T(8,128)(2,1)S(1)} %get-tuple-element.29), channel_id=1, replica_groups={{0,16,32,48,64,80,96,112,128,144,160,176,192,208,224,240},{8,24,40,56,7..., dimensions={0} | all-to-all | bytes 2097152 | tf_op jit(solution)/shard_map/all_to_all | solution.py:208
  73.8 1.6 shard_map.77
  75.4 18.8 %all_to_all.83.terms = bf16[8,2,128,128]{3,2,1,0:T(8,128)(2,1)S(1)} all-to-all(bf16[8,2,128,128]{3,2,1,0:T(8,128)(2,1)S(1)} %shard_map.77), channel_id=1, replica_groups=mesh['prow'=32,'pcol'=8] {'pcol'}, dimensions={0} | all-to-all | bytes 1048576 | tf_op jit(solution)/shard_map/all_to_all | solution.py:212
  94.5 16.1 %all_to_all.84 = bf16[16,2,128,128]{3,2,1,0:T(8,128)(2,1)S(1)} all-to-all(bf16[16,2,128,128]{3,2,1,0:T(8,128)(2,1)S(1)} %get-tuple-element.30), channel_id=1, replica_groups={{0,16,32,48,64,80,96,112,128,144,160,176,192,208,224,240},{8,24,40,56,7..., dimensions={0} | all-to-all | bytes 2097152 | tf_op jit(solution)/shard_map/all_to_all | solution.py:208
  112.5 19.2 %all_to_all.85.terms = bf16[8,2,128,128]{3,2,1,0:T(8,128)(2,1)S(1)} all-to-all(bf16[8,2,128,128]{3,2,1,0:T(8,128)(2,1)S(1)} %shard_map.79), channel_id=1, replica_groups=mesh['prow'=32,'pcol'=8] {'pcol'}, dimensions={0} | all-to-all | bytes 1048576 | tf_op jit(solution)/shard_map/all_to_all | solution.py:212
  132.0 15.0 %all_to_all.86 = bf16[16,2,128,128]{3,2,1,0:T(8,128)(2,1)S(1)} all-to-all(bf16[16,2,128,128]{3,2,1,0:T(8,128)(2,1)S(1)} %get-tuple-element.31), channel_id=1, replica_groups={{0,16,32,48,64,80,96,112,128,144,160,176,192,208,224,240},{8,24,40,56,7..., dimensions={0} | all-to-all | bytes 2097152 | tf_op jit(solution)/shard_map/all_to_all | solution.py:208
  149.1 19.4 %all_to_all.87.terms = bf16[8,2,128,128]{3,2,1,0:T(8,128)(2,1)S(1)} all-to-all(bf16[8,2,128,128]{3,2,1,0:T(8,128)(2,1)S(1)} %shard_map.81), channel_id=1, replica_groups=mesh['prow'=32,'pcol'=8] {'pcol'}, dimensions={0} | all-to-all | bytes 1048576 | tf_op jit(solution)/shard_map/all_to_all | solution.py:212
  168.9 15.5 %all_to_all.88 = bf16[16,2,128,128]{3,2,1,0:T(8,128)(2,1)S(1)} all-to-all(bf16[16,2,128,128]{3,2,1,0:T(8,128)(2,1)S(1)} %get-tuple-element.32), channel_id=1, replica_groups={{0,16,32,48,64,80,96,112,128,144,160,176,192,208,224,240},{8,24,40,56,7..., dimensions={0} | all-to-all | bytes 2097152 | tf_op jit(solution)/shard_map/all_to_all | solution.py:208
  184.5 1.6 shard_map.83
  186.1 18.3 %all_to_all.89.terms = bf16[8,2,128,128]{3,2,1,0:T(8,128)(2,1)S(1)} all-to-all(bf16[8,2,128,128]{3,2,1,0:T(8,128)(2,1)S(1)} %shard_map.83), channel_id=1, replica_groups=mesh['prow'=32,'pcol'=8] {'pcol'}, dimensions={0} | all-to-all | bytes 1048576 | tf_op jit(solution)/shard_map/all_to_all | solution.py:212
  204.6 15.5 %all_to_all.90 = bf16[16,2,128,128]{3,2,1,0:T(8,128)(2,1)S(1)} all-to-all(bf16[16,2,128,128]{3,2,1,0:T(8,128)(2,1)S(1)} %get-tuple-element.34), channel_id=1, replica_groups={{0,16,32,48,64,80,96,112,128,144,160,176,192,208,224,240},{8,24,40,56,7..., dimensions={0} | all-to-all | bytes 2097152 | tf_op jit(solution)/shard_map/all_to_all | solution.py:208
  220.3 1.6 shard_map.85
  221.9 19.1 %all_to_all.91.terms = bf16[8,2,128,128]{3,2,1,0:T(8,128)(2,1)S(1)} all-to-all(bf16[8,2,128,128]{3,2,1,0:T(8,128)(2,1)S(1)} %shard_map.85), channel_id=1, replica_groups=mesh['prow'=32,'pcol'=8] {'pcol'}, dimensions={0} | all-to-all | bytes 1048576 | tf_op jit(solution)/shard_map/all_to_all | solution.py:212
  241.3 15.1 %all_to_all.92 = bf16[16,2,128,128]{3,2,1,0:T(8,128)(2,1)S(1)} all-to-all(bf16[16,2,128,128]{3,2,1,0:T(8,128)(2,1)S(1)} %get-tuple-element.36), channel_id=1, replica_groups={{0,16,32,48,64,80,96,112,128,144,160,176,192,208,224,240},{8,24,40,56,7..., dimensions={0} | all-to-all | bytes 2097152 | tf_op jit(solution)/shard_map/all_to_all | solution.py:208
  256.7 1.6 shard_map.87
  258.3 19.0 %all_to_all.93.terms = bf16[8,2,128,128]{3,2,1,0:T(8,128)(2,1)S(1)} all-to-all(bf16[8,2,128,128]{3,2,1,0:T(8,128)(2,1)S(1)} %shard_map.87), channel_id=1, replica_groups=mesh['prow'=32,'pcol'=8] {'pcol'}, dimensions={0} | all-to-all | bytes 1048576 | tf_op jit(solution)/shard_map/all_to_all | solution.py:212
  277.6 14.9 %all_to_all.94 = bf16[16,2,128,128]{3,2,1,0:T(8,128)(2,1)S(1)} all-to-all(bf16[16,2,128,128]{3,2,1,0:T(8,128)(2,1)S(1)} %get-tuple-element.38), channel_id=1, replica_groups={{0,16,32,48,64,80,96,112,128,144,160,176,192,208,224,240},{8,24,40,56,7..., dimensions={0} | all-to-all | bytes 2097152 | tf_op jit(solution)/shard_map/all_to_all | solution.py:208
  293.0 1.6 shard_map.89
  294.6 17.9 %all_to_all.95.terms = bf16[8,2,128,128]{3,2,1,0:T(8,128)(2,1)S(1)} all-to-all(bf16[8,2,128,128]{3,2,1,0:T(8,128)(2,1)S(1)} %shard_map.89), channel_id=1, replica_groups=mesh['prow'=32,'pcol'=8] {'pcol'}, dimensions={0} | all-to-all | bytes 1048576 | tf_op jit(solution)/shard_map/all_to_all | solution.py:212
  312.8 6.1 %collective-permute-start.4 = (bf16[5,128,128]{2,1,0:T(8,128)(2,1)S(1)}, bf16[5,128,128]{2,1,0:T(8,128)(2,1)S(1)}, u32[]{:S(2)}, u32[]{:S(2)}) collective-permute-start(bf16[5,128,128]{2,1,0:T(8,128)(2,1)S(1)} %slice_bitcast_fusion), channel_id=1, source_target_pairs={{0,8},{8,0},{16,24},{24,16},{32,40},{40,32},{48,56},{56,48},{64,72... | collective-permute-start | bytes 491528 | tf_op jit(solution)/shard_map/ppermute | solution.py:193
  (48 shorter events, 13.9 us)
Async XLA Ops:
  1.4 5.6 %collective-permute-start.1 = (bf16[16,128,128]{2,1,0:T(8,128)(2,1)S(1)}, bf16[16,128,128]{2,1,0:T(8,128)(2,1)S(1)}, u32[]{:S(2)}, u32[]{:S(2)}) collective-permute-start(bf16[16,128,128]{2,1,0:T(8,128)(2,1)S(1)} %get-tuple-element.24), channel_id=1, source_target_pairs={{0,8},{8,0},{16,24},{24,16},{32,40},{40,32},{48,56},{56,48},{64,72... | collective-permute-start | bytes 1572872 | tf_op jit(solution)/shard_map/ppermute | solution.py:193
  5.7 1.2 collective-permute-start
  6.9 22.1 %collective-permute-start.3 = (bf16[4,8,6,128,128]{4,3,2,1,0:T(8,128)(2,1)}, bf16[4,8,6,128,128]{4,3,2,1,0:T(8,128)(2,1)S(1)}, u32[]{:S(2)}, u32[]{:S(2)}) collective-permute-start(bf16[4,8,6,128,128]{4,3,2,1,0:T(8,128)(2,1)} %own.11), channel_id=1, source_target_pairs={{0,8},{8,0},{16,24},{24,16},{32,40},{40,32},{48,56},{56,48},{64,72... | collective-permute-start | bytes 18874376 | tf_op jit(solution)/shard_map/ppermute | solution.py:193
  7.2 66.6 %collective-permute-start.2 = (bf16[4,8,6,128,128]{4,3,2,1,0:T(8,128)(2,1)}, bf16[4,8,6,128,128]{4,3,2,1,0:T(8,128)(2,1)S(1)}, u32[]{:S(2)}, u32[]{:S(2)}) collective-permute-start(bf16[4,8,6,128,128]{4,3,2,1,0:T(8,128)(2,1)} %own.15), channel_id=1, source_target_pairs={{0,8},{8,0},{16,24},{24,16},{32,40},{40,32},{48,56},{56,48},{64,72... | collective-permute-start | bytes 18874376 | tf_op jit(solution)/shard_map/ppermute | solution.py:193
  29.0 44.8 %slice-start.2 = ((s8[6291456]{0:T(1024)(128)(4,1)}), s8[4194304]{0:T(1024)(128)(4,1)S(1)}, s32[]{:S(2)}) async-start(s8[6291456]{0:T(1024)(128)(4,1)} %bitcast.39), calls=%async_computation.18 | async-start | bytes 8388608
  29.0 44.8 %slice-start.3 = ((s8[6291456]{0:T(1024)(128)(4,1)}), s8[2097152]{0:T(1024)(128)(4,1)S(1)}, s32[]{:S(2)}) async-start(s8[6291456]{0:T(1024)(128)(4,1)} %bitcast.39), calls=%async_computation.19 | async-start | bytes 4194304
  147.0 37.5 %slice-start = ((s8[6291456]{0:T(1024)(128)(4,1)}), s8[4194304]{0:T(1024)(128)(4,1)S(1)}, s32[]{:S(2)}) async-start(s8[6291456]{0:T(1024)(128)(4,1)} %bitcast.37), calls=%async_computation.16 | async-start | bytes 8388608
  147.6 36.9 %slice-start.1 = ((s8[6291456]{0:T(1024)(128)(4,1)}), s8[2097152]{0:T(1024)(128)(4,1)S(1)}, s32[]{:S(2)}) async-start(s8[6291456]{0:T(1024)(128)(4,1)} %bitcast.37), calls=%async_computation.17 | async-start | bytes 4194304
  312.8 7.2 %collective-permute-start.4 = (bf16[5,128,128]{2,1,0:T(8,128)(2,1)S(1)}, bf16[5,128,128]{2,1,0:T(8,128)(2,1)S(1)}, u32[]{:S(2)}, u32[]{:S(2)}) collective-permute-start(bf16[5,128,128]{2,1,0:T(8,128)(2,1)S(1)} %slice_bitcast_fusion), channel_id=1, source_target_pairs={{0,8},{8,0},{16,24},{24,16},{32,40},{40,32},{48,56},{56,48},{64,72... | collective-permute-start | bytes 491528 | tf_op jit(solution)/shard_map/ppermute | solution.py:193

commit v3 on v2

--- a/solution.py
+++ b/solution.py
@@ -188,6 +188,12 @@
     mates = [(i, i ^ 1) for i in range(n_prow)]
     planes = [[i * 2 + c for i in range(n_prow // 2)] for c in range(2)]
     copies = n_prow // 2
+    n_pcol = lax.axis_size("pcol")
+    behind = [
+        (i * n_pcol + k, i * n_pcol + (k + 1) % n_pcol)
+        for i in range(1, n_prow, 2)
+        for k in range(n_pcol)
+    ]
 
     def swap(x):
         return lax.ppermute(x, "prow", mates)
@@ -204,6 +210,10 @@
     )
     lower_mate, upper_mate = swap(lower_given), swap(upper_given)
 
+    token = got[3 * levels, :16]
+    for _ in range(5):
+        token = lax.ppermute(token, ("prow", "pcol"), behind) + kept[:16]
+
     def heard(sent):
         got = lax.all_to_all(sent, "prow", 0, 0, axis_index_groups=planes)
         return got.reshape(n_prow, width, half)
@@ -211,7 +221,7 @@
     def collect(x):
         return lax.all_to_all(x, "pcol", 0, 0)
 
-    sent = spread_call(copies, kept, got, [numbers])
+    sent = spread_call(copies, kept, got, [numbers, token])
     low, pieces = [(kept, got)], [heard(sent)]
     for height in range(1, levels):
         sums = row_sums(

time: 322 us -> 300 us (0.932)
  blocking collectives: 286 us -> 241 us
  waiting for transfers between devices: 2.18 us -> 22.2 us
  starting transfers between devices: 10.2 us -> 13.7 us
    all_to_all x8, blocking collectives: 154 us -> 121 us  [collect(): return lax.all_to_all(x, 'pcol', 0, 0)]
    ppermute x0 -> x5, waiting for transfers between devices: none -> 19.6 us  [shards(): token = lax.ppermute(token, ('prow', 'pcol'), behind) + kept[:16]]
    all_to_all x8, blocking collectives: 132 us -> 120 us  [heard(): got = lax.all_to_all(sent, 'prow', 0, 0, axis_index_groups=planes)]
    ppermute x0 -> x5, starting transfers between devices: none -> 9.54 us  [shards(): token = lax.ppermute(token, ('prow', 'pcol'), behind) + kept[:16]]
    ppermute x5, starting transfers between devices: 10.2 us -> 4.12 us  [swap(): return lax.ppermute(x, 'prow', mates)]
  transfers between devices with their start and end apart: 5 -> 10, of which waited for: 2 -> 7; matrix products, arithmetic and copies ran while one was open for 0% -> 0% of each run, Pallas kernels for 1% -> 1%
where the time goes in v3:
time: 300 us; the launch traced here: 299 us
  blocking collectives  241 us (80%)
  waiting for transfers between devices  22.2 us (7%)
  Pallas kernels  18.3 us (6%)
  starting transfers between devices  13.7 us (5%)
  other arithmetic  3.74 us (1%)
    all_to_all x8, blocking collectives, collect(): return lax.all_to_all(x, 'pcol', 0, 0)  121 us
    all_to_all x8, blocking collectives, heard(): got = lax.all_to_all(sent, 'prow', 0, 0, axis_index_groups=planes)  120 us
    ppermute x5, waiting for transfers between devices, shards(): token = lax.ppermute(token, ('prow', 'pcol'), behind) + kept[:16]  19.6 us
    pallas_call x8, Pallas kernels, row_sums(): pl.pallas_call(functools.partial(rows_kernel, level, base, which, fetch),...  14.4 us
    ppermute x5, starting transfers between devices, shards(): token = lax.ppermute(token, ('prow', 'pcol'), behind) + kept[:16]  9.54 us
  transfers between devices with their start and end apart: 10, of which 7 were waited for; matrix products, arithmetic and copies ran while one was open for 0% of the time, Pallas kernels for 1%

profile of v3, /device:TPU:1, one launch (start us, length us, event | category | flops | bytes accessed | tf_op | source)
XLA Modules:
  0.0 299.1 jit_solution(11474290268880641323)
XLA Ops:
  1.4 3.3 %collective-permute-start.1 = (bf16[16,128,128]{2,1,0:T(8,128)(2,1)S(1)}, bf16[16,128,128]{2,1,0:T(8,128)(2,1)S(1)}, u32[]{:S(2)}, u32[]{:S(2)}) collective-permute-start(bf16[16,128,128]{2,1,0:T(8,128)(2,1)S(1)} %get-tuple-element.24), channel_id=1, source_target_pairs={{0,8},{8,0},{16,24},{24,16},{32,40},{40,32},{48,56},{56,48},{64,72... | collective-permute-start | bytes 1572872 | tf_op jit(solution)/shard_map/ppermute | solution.py:199
  9.5 4.8 %collective-permute-done.4 = bf16[16,128]{1,0:T(8,128)(2,1)S(1)} collective-permute-done((bf16[16,128]{1,0:T(8,128)(2,1)S(1)}, bf16[16,128]{1,0:T(8,128)(2,1)S(1)}, u32[]{:S(2)}, u32[]{:S(2)}) %collective-permute-start.4) | collective-permute-done | bytes 4128 | tf_op jit(solution)/shard_map/ppermute | solution.py:215
  14.3 1.9 collective-permute-start.5
  16.2 3.6 %collective-permute-done.5 = bf16[16,128]{1,0:T(8,128)(2,1)S(1)} collective-permute-done((bf16[16,128]{1,0:T(8,128)(2,1)S(1)}, bf16[16,128]{1,0:T(8,128)(2,1)S(1)}, u32[]{:S(2)}, u32[]{:S(2)}) %collective-permute-start.5) | collective-permute-done | bytes 4128 | tf_op jit(solution)/shard_map/ppermute | solution.py:215
  21.7 3.9 %collective-permute-done.6 = bf16[16,128]{1,0:T(8,128)(2,1)S(1)} collective-permute-done((bf16[16,128]{1,0:T(8,128)(2,1)S(1)}, bf16[16,128]{1,0:T(8,128)(2,1)S(1)}, u32[]{:S(2)}, u32[]{:S(2)}) %collective-permute-start.6) | collective-permute-done | bytes 4128 | tf_op jit(solution)/shard_map/ppermute | solution.py:215
  27.6 3.6 %collective-permute-done.7 = bf16[16,128]{1,0:T(8,128)(2,1)S(1)} collective-permute-done((bf16[16,128]{1,0:T(8,128)(2,1)S(1)}, bf16[16,128]{1,0:T(8,128)(2,1)S(1)}, u32[]{:S(2)}, u32[]{:S(2)}) %collective-permute-start.7) | collective-permute-done | bytes 4128 | tf_op jit(solution)/shard_map/ppermute | solution.py:215
  33.2 3.6 %collective-permute-done.8 = bf16[16,128]{1,0:T(8,128)(2,1)S(1)} collective-permute-done((bf16[16,128]{1,0:T(8,128)(2,1)S(1)}, bf16[16,128]{1,0:T(8,128)(2,1)S(1)}, u32[]{:S(2)}, u32[]{:S(2)}) %collective-permute-start.8) | collective-permute-done | bytes 4128 | tf_op jit(solution)/shard_map/ppermute | solution.py:215
  36.9 18.4 %all_to_all.80 = bf16[16,2,128,128]{3,2,1,0:T(8,128)(2,1)S(1)} all-to-all(bf16[16,2,128,128]{3,2,1,0:T(8,128)(2,1)S(1)} %shard_map.74), channel_id=1, replica_groups={{0,16,32,48,64,80,96,112,128,144,160,176,192,208,224,240},{8,24,40,56,7..., dimensions={0} | all-to-all | bytes 2097152 | tf_op jit(solution)/shard_map/all_to_all | solution.py:218
  55.3 3.4 %shard_map.75 = bf16[8,2,128,128]{3,2,1,0:T(8,128)(2,1)S(1)} custom-call(s32[768]{0:T(1024)S(1)} %add_xor_fusion.rest_0_.numbers, bf16[4,8,6,128,128]{4,3,2,1,0:T(8,128)(2,1)} %own.11, bf16[4,8,6,128,128]{4,3,2,1,0:T(8,128)(2,1)S(1)} %collective-permute-done.3.mate, bf16[32,128,128]{2,1,0:T(8,128)(2,1)S(1)} %bitcast.43), custom_call_target="tpu_custom_call" | custom-call | tf_op jit(solution)/shard_map/pallas_call | solution.py:160
  58.8 17.2 %all_to_all.81.terms = bf16[8,2,128,128]{3,2,1,0:T(8,128)(2,1)S(1)} all-to-all(bf16[8,2,128,128]{3,2,1,0:T(8,128)(2,1)S(1)} %shard_map.75), channel_id=1, replica_groups=mesh['prow'=32,'pcol'=8] {'pcol'}, dimensions={0} | all-to-all | bytes 1048576 | tf_op jit(solution)/shard_map/all_to_all | solution.py:222
  76.3 14.5 %all_to_all.82 = bf16[16,2,128,128]{3,2,1,0:T(8,128)(2,1)S(1)} all-to-all(bf16[16,2,128,128]{3,2,1,0:T(8,128)(2,1)S(1)} %get-tuple-element.29), channel_id=1, replica_groups={{0,16,32,48,64,80,96,112,128,144,160,176,192,208,224,240},{8,24,40,56,7..., dimensions={0} | all-to-all | bytes 2097152 | tf_op jit(solution)/shard_map/all_to_all | solution.py:218
  92.6 14.5 %all_to_all.83.terms = bf16[8,2,128,128]{3,2,1,0:T(8,128)(2,1)S(1)} all-to-all(bf16[8,2,128,128]{3,2,1,0:T(8,128)(2,1)S(1)} %shard_map.77), channel_id=1, replica_groups=mesh['prow'=32,'pcol'=8] {'pcol'}, dimensions={0} | all-to-all | bytes 1048576 | tf_op jit(solution)/shard_map/all_to_all | solution.py:222
  107.4 14.5 %all_to_all.84 = bf16[16,2,128,128]{3,2,1,0:T(8,128)(2,1)S(1)} all-to-all(bf16[16,2,128,128]{3,2,1,0:T(8,128)(2,1)S(1)} %get-tuple-element.30), channel_id=1, replica_groups={{0,16,32,48,64,80,96,112,128,144,160,176,192,208,224,240},{8,24,40,56,7..., dimensions={0} | all-to-all | bytes 2097152 | tf_op jit(solution)/shard_map/all_to_all | solution.py:218
  123.8 14.5 %all_to_all.85.terms = bf16[8,2,128,128]{3,2,1,0:T(8,128)(2,1)S(1)} all-to-all(bf16[8,2,128,128]{3,2,1,0:T(8,128)(2,1)S(1)} %shard_map.79), channel_id=1, replica_groups=mesh['prow'=32,'pcol'=8] {'pcol'}, dimensions={0} | all-to-all | bytes 1048576 | tf_op jit(solution)/shard_map/all_to_all | solution.py:222
  138.7 14.5 %all_to_all.86 = bf16[16,2,128,128]{3,2,1,0:T(8,128)(2,1)S(1)} all-to-all(bf16[16,2,128,128]{3,2,1,0:T(8,128)(2,1)S(1)} %get-tuple-element.31), channel_id=1, replica_groups={{0,16,32,48,64,80,96,112,128,144,160,176,192,208,224,240},{8,24,40,56,7..., dimensions={0} | all-to-all | bytes 2097152 | tf_op jit(solution)/shard_map/all_to_all | solution.py:218
  155.3 14.8 %all_to_all.87.terms = bf16[8,2,128,128]{3,2,1,0:T(8,128)(2,1)S(1)} all-to-all(bf16[8,2,128,128]{3,2,1,0:T(8,128)(2,1)S(1)} %shard_map.81), channel_id=1, replica_groups=mesh['prow'=32,'pcol'=8] {'pcol'}, dimensions={0} | all-to-all | bytes 1048576 | tf_op jit(solution)/shard_map/all_to_all | solution.py:222
  170.5 14.5 %all_to_all.88 = bf16[16,2,128,128]{3,2,1,0:T(8,128)(2,1)S(1)} all-to-all(bf16[16,2,128,128]{3,2,1,0:T(8,128)(2,1)S(1)} %get-tuple-element.32), channel_id=1, replica_groups={{0,16,32,48,64,80,96,112,128,144,160,176,192,208,224,240},{8,24,40,56,7..., dimensions={0} | all-to-all | bytes 2097152 | tf_op jit(solution)/shard_map/all_to_all | solution.py:218
  186.6 14.8 %all_to_all.89.terms = bf16[8,2,128,128]{3,2,1,0:T(8,128)(2,1)S(1)} all-to-all(bf16[8,2,128,128]{3,2,1,0:T(8,128)(2,1)S(1)} %shard_map.83), channel_id=1, replica_groups=mesh['prow'=32,'pcol'=8] {'pcol'}, dimensions={0} | all-to-all | bytes 1048576 | tf_op jit(solution)/shard_map/all_to_all | solution.py:222
  201.7 14.5 %all_to_all.90 = bf16[16,2,128,128]{3,2,1,0:T(8,128)(2,1)S(1)} all-to-all(bf16[16,2,128,128]{3,2,1,0:T(8,128)(2,1)S(1)} %get-tuple-element.34), channel_id=1, replica_groups={{0,16,32,48,64,80,96,112,128,144,160,176,192,208,224,240},{8,24,40,56,7..., dimensions={0} | all-to-all | bytes 2097152 | tf_op jit(solution)/shard_map/all_to_all | solution.py:218
  218.0 14.5 %all_to_all.91.terms = bf16[8,2,128,128]{3,2,1,0:T(8,128)(2,1)S(1)} all-to-all(bf16[8,2,128,128]{3,2,1,0:T(8,128)(2,1)S(1)} %shard_map.85), channel_id=1, replica_groups=mesh['prow'=32,'pcol'=8] {'pcol'}, dimensions={0} | all-to-all | bytes 1048576 | tf_op jit(solution)/shard_map/all_to_all | solution.py:222
  232.8 14.5 %all_to_all.92 = bf16[16,2,128,128]{3,2,1,0:T(8,128)(2,1)S(1)} all-to-all(bf16[16,2,128,128]{3,2,1,0:T(8,128)(2,1)S(1)} %get-tuple-element.36), channel_id=1, replica_groups={{0,16,32,48,64,80,96,112,128,144,160,176,192,208,224,240},{8,24,40,56,7..., dimensions={0} | all-to-all | bytes 2097152 | tf_op jit(solution)/shard_map/all_to_all | solution.py:218
  249.2 14.5 %all_to_all.93.terms = bf16[8,2,128,128]{3,2,1,0:T(8,128)(2,1)S(1)} all-to-all(bf16[8,2,128,128]{3,2,1,0:T(8,128)(2,1)S(1)} %shard_map.87), channel_id=1, replica_groups=mesh['prow'=32,'pcol'=8] {'pcol'}, dimensions={0} | all-to-all | bytes 1048576 | tf_op jit(solution)/shard_map/all_to_all | solution.py:222
  264.1 14.4 %all_to_all.94 = bf16[16,2,128,128]{3,2,1,0:T(8,128)(2,1)S(1)} all-to-all(bf16[16,2,128,128]{3,2,1,0:T(8,128)(2,1)S(1)} %get-tuple-element.38), channel_id=1, replica_groups={{0,16,32,48,64,80,96,112,128,144,160,176,192,208,224,240},{8,24,40,56,7..., dimensions={0} | all-to-all | bytes 2097152 | tf_op jit(solution)/shard_map/all_to_all | solution.py:218
  280.6 15.9 %all_to_all.95.terms = bf16[8,2,128,128]{3,2,1,0:T(8,128)(2,1)S(1)} all-to-all(bf16[8,2,128,128]{3,2,1,0:T(8,128)(2,1)S(1)} %shard_map.89), channel_id=1, replica_groups=mesh['prow'=32,'pcol'=8] {'pcol'}, dimensions={0} | all-to-all | bytes 1048576 | tf_op jit(solution)/shard_map/all_to_all | solution.py:222
  (64 shorter events, 29.9 us)
Async XLA Ops:
  1.4 5.6 %collective-permute-start.1 = (bf16[16,128,128]{2,1,0:T(8,128)(2,1)S(1)}, bf16[16,128,128]{2,1,0:T(8,128)(2,1)S(1)}, u32[]{:S(2)}, u32[]{:S(2)}) collective-permute-start(bf16[16,128,128]{2,1,0:T(8,128)(2,1)S(1)} %get-tuple-element.24), channel_id=1, source_target_pairs={{0,8},{8,0},{16,24},{24,16},{32,40},{40,32},{48,56},{56,48},{64,72... | collective-permute-start | bytes 1572872 | tf_op jit(solution)/shard_map/ppermute | solution.py:199
  5.7 1.2 collective-permute-start
  6.9 48.4 %collective-permute-start.3 = (bf16[4,8,6,128,128]{4,3,2,1,0:T(8,128)(2,1)}, bf16[4,8,6,128,128]{4,3,2,1,0:T(8,128)(2,1)S(1)}, u32[]{:S(2)}, u32[]{:S(2)}) collective-permute-start(bf16[4,8,6,128,128]{4,3,2,1,0:T(8,128)(2,1)} %own.11), channel_id=1, source_target_pairs={{0,8},{8,0},{16,24},{24,16},{32,40},{40,32},{48,56},{56,48},{64,72... | collective-permute-start | bytes 18874376 | tf_op jit(solution)/shard_map/ppermute | solution.py:199
  7.2 83.8 %collective-permute-start.2 = (bf16[4,8,6,128,128]{4,3,2,1,0:T(8,128)(2,1)}, bf16[4,8,6,128,128]{4,3,2,1,0:T(8,128)(2,1)S(1)}, u32[]{:S(2)}, u32[]{:S(2)}) collective-permute-start(bf16[4,8,6,128,128]{4,3,2,1,0:T(8,128)(2,1)} %own.15), channel_id=1, source_target_pairs={{0,8},{8,0},{16,24},{24,16},{32,40},{40,32},{48,56},{56,48},{64,72... | collective-permute-start | bytes 18874376 | tf_op jit(solution)/shard_map/ppermute | solution.py:199
  7.5 6.7 %collective-permute-start.4 = (bf16[16,128]{1,0:T(8,128)(2,1)S(1)}, bf16[16,128]{1,0:T(8,128)(2,1)S(1)}, u32[]{:S(2)}, u32[]{:S(2)}) collective-permute-start(bf16[16,128]{1,0:T(8,128)(2,1)S(1)} %slice_bitcast_fusion.2), channel_id=1, source_target_pairs={{8,9},{9,10},{10,11},{11,12},{12,13},{13,14},{14,15},{15,8},{24,25... | collective-permute-start | bytes 12296 | tf_op jit(solution)/shard_map/ppermute | solution.py:215
  14.3 5.6 %collective-permute-start.5 = (bf16[16,128]{1,0:T(8,128)(2,1)S(1)}, bf16[16,128]{1,0:T(8,128)(2,1)S(1)}, u32[]{:S(2)}, u32[]{:S(2)}) collective-permute-start(bf16[16,128]{1,0:T(8,128)(2,1)S(1)} %slice_add_fusion.4), channel_id=1, source_target_pairs={{8,9},{9,10},{10,11},{11,12},{12,13},{13,14},{14,15},{15,8},{24,25... | collective-permute-start | bytes 12296 | tf_op jit(solution)/shard_map/ppermute | solution.py:215
  19.8 5.8 %collective-permute-start.6 = (bf16[16,128]{1,0:T(8,128)(2,1)S(1)}, bf16[16,128]{1,0:T(8,128)(2,1)S(1)}, u32[]{:S(2)}, u32[]{:S(2)}) collective-permute-start(bf16[16,128]{1,0:T(8,128)(2,1)S(1)} %slice_add_fusion.3), channel_id=1, source_target_pairs={{8,9},{9,10},{10,11},{11,12},{12,13},{13,14},{14,15},{15,8},{24,25... | collective-permute-start | bytes 12296 | tf_op jit(solution)/shard_map/ppermute | solution.py:215
  25.7 5.6 %collective-permute-start.7 = (bf16[16,128]{1,0:T(8,128)(2,1)S(1)}, bf16[16,128]{1,0:T(8,128)(2,1)S(1)}, u32[]{:S(2)}, u32[]{:S(2)}) collective-permute-start(bf16[16,128]{1,0:T(8,128)(2,1)S(1)} %slice_add_fusion.2), channel_id=1, source_target_pairs={{8,9},{9,10},{10,11},{11,12},{12,13},{13,14},{14,15},{15,8},{24,25... | collective-permute-start | bytes 12296 | tf_op jit(solution)/shard_map/ppermute | solution.py:215
  31.2 5.6 %collective-permute-start.8 = (bf16[16,128]{1,0:T(8,128)(2,1)S(1)}, bf16[16,128]{1,0:T(8,128)(2,1)S(1)}, u32[]{:S(2)}, u32[]{:S(2)}) collective-permute-start(bf16[16,128]{1,0:T(8,128)(2,1)S(1)} %slice_add_fusion.1), channel_id=1, source_target_pairs={{8,9},{9,10},{10,11},{11,12},{12,13},{13,14},{14,15},{15,8},{24,25... | collective-permute-start | bytes 12296 | tf_op jit(solution)/shard_map/ppermute | solution.py:215
  55.3 35.6 %slice-start.2 = ((s8[6291456]{0:T(1024)(128)(4,1)}), s8[4194304]{0:T(1024)(128)(4,1)S(1)}, s32[]{:S(2)}) async-start(s8[6291456]{0:T(1024)(128)(4,1)} %bitcast.41), calls=%async_computation.18 | async-start | bytes 8388608
  55.3 35.6 %slice-start.3 = ((s8[6291456]{0:T(1024)(128)(4,1)}), s8[2097152]{0:T(1024)(128)(4,1)S(1)}, s32[]{:S(2)}) async-start(s8[6291456]{0:T(1024)(128)(4,1)} %bitcast.41), calls=%async_computation.19 | async-start | bytes 4194304
  153.1 31.9 %slice-start = ((s8[6291456]{0:T(1024)(128)(4,1)}), s8[4194304]{0:T(1024)(128)(4,1)S(1)}, s32[]{:S(2)}) async-start(s8[6291456]{0:T(1024)(128)(4,1)} %bitcast.39), calls=%async_computation.16 | async-start | bytes 8388608
  153.7 31.3 %slice-start.1 = ((s8[6291456]{0:T(1024)(128)(4,1)}), s8[2097152]{0:T(1024)(128)(4,1)S(1)}, s32[]{:S(2)}) async-start(s8[6291456]{0:T(1024)(128)(4,1)} %bitcast.39), calls=%async_computation.17 | async-start | bytes 4194304
  296.8 1.5 collective-permute-start.9

commit v4 on v3

v4 whole, which is shorter than its diff:
```python
import functools

import jax
import jax.numpy as jnp
from jax import lax
from jax.experimental import pallas as pl
from jax.experimental.pallas import tpu as pltpu
from jax.sharding import PartitionSpec as P

F32 = jnp.float32
BF16 = jnp.bfloat16


def first_kernel(core, side, lower, upper, blocks, mine, given, near, *scratch):
    levels, _, width, columns = side.shape
    held, sems = scratch[:3], scratch[3]
    half = columns // 2
    cut = near.shape[1] // 2

    def copy(i):
        if i < 3:
            return pltpu.make_async_copy((side, lower, upper)[i], held[i], sems.at[i])
        part = pl.ds((i - 3) * cut, cut)
        return pltpu.make_async_copy(blocks.at[0, part], near.at[0, part], sems.at[i])

    for i in range(5):
        copy(i).start()
    for i in range(3):
        copy(i).wait()
    here = pl.ds(pl.multiple_of(core[0] * half, half), half)
    there = pl.ds(pl.multiple_of((1 - core[0]) * half, half), half)
    sides, lowers, uppers = held
    for out, part in ((given, there), (mine, here)):
        for level in range(levels):
            out[level] = lowers[level, 0]
            out[levels + level] = uppers[level, 0]
            out[2 * levels + level] = sides[level, 0, :, part]
        out[3 * levels] = jnp.dot(
            lowers[0, 0], sides[0, 0, :, part], preferred_element_type=F32
        ).astype(BF16)
    for i in range(3, 5):
        copy(i).wait()


def first_call(core, *arrays):
    levels, _, width, columns = arrays[0].shape
    packed = jax.ShapeDtypeStruct((3 * levels + 1, width, columns // 2), BF16)
    near = jax.ShapeDtypeStruct((1,) + arrays[3].shape[1:], BF16)
    arrays = [pltpu.with_memory_space_constraint(x, pltpu.HBM) for x in arrays]
    return pl.pallas_call(
        first_kernel,
        grid_spec=pltpu.PrefetchScalarGridSpec(
            num_scalar_prefetch=1,
            grid=(1,),
            in_specs=[pl.BlockSpec(memory_space=pltpu.HBM)] * 4,
            out_specs=[pl.BlockSpec(memory_space=pltpu.VMEM)] * 3,
            scratch_shapes=[pltpu.VMEM(x.shape, BF16) for x in arrays[:3]]
            + [pltpu.SemaphoreType.DMA((5,))],
        ),
        out_shape=[packed, packed, near],
        compiler_params=pltpu.CompilerParams(vmem_limit_bytes=16 << 20),
    )(core, *arrays)


def spread_kernel(mine, got, *rest):
    out = rest[-1]
    last = got.shape[0] - 1
    for i in range(out.shape[0]):
        out[i, 0] = mine[last]
        out[i, 1] = got[last]


def spread_call(copies, mine, got, others):
    shape = (copies, 2) + got.shape[1:]
    return pl.pallas_call(
        spread_kernel,
        in_specs=[pl.BlockSpec(memory_space=pltpu.VMEM)] * 2
        + [pl.BlockSpec(memory_space=pl.ANY)] * len(others),
        out_specs=pl.BlockSpec(memory_space=pltpu.VMEM),
        out_shape=jax.ShapeDtypeStruct(shape, BF16),
        compiler_params=pltpu.CompilerParams(vmem_limit_bytes=16 << 20),
    )(mine, got, *others)


def remain_of(terms, slot, side):
    total = terms[0, slot].astype(F32)
    for source in range(1, terms.shape[0]):
        total += terms[source, slot].astype(F32)
    return (side.astype(F32) - total).astype(BF16)


def solve_kernel(picks, terms, mine, got, *refs):
    side_pick, inverse_picks, n_before = picks
    before, outs = refs[:n_before], refs[n_before:]
    for slot, packed in enumerate((mine, got)):
        side = before[0][slot] if before else packed[side_pick]
        x = remain_of(terms, slot, side)
        for pick in inverse_picks:
            x = jnp.dot(packed[pick], x, preferred_element_type=F32).astype(BF16)
        outs[0][slot] = x
        for sent in outs[1:]:
            for i in range(sent.shape[0]):
                sent[i, slot] = x


def solve_call(side_pick, inverse_picks, copies, terms, mine, got, before=()):
    _, pair, width, half = terms.shape
    outs = [jax.ShapeDtypeStruct((pair, width, half), BF16)]
    if copies:
        outs.append(jax.ShapeDtypeStruct((copies, pair, width, half), BF16))
    vmem = pl.BlockSpec(memory_space=pltpu.VMEM)
    return pl.pallas_call(
        functools.partial(solve_kernel, (side_pick, inverse_picks, len(before))),
        in_specs=[vmem] * (3 + len(before)),
        out_specs=[vmem] * len(outs),
        out_shape=outs,
        compiler_params=pltpu.CompilerParams(vmem_limit_bytes=16 << 20),
    )(terms, mine, got, *before)


def rows_kernel(level, base, which, numbers, own, mate, stored, *rest):
    levels, rows, per_row = mate.shape[:3]
    out = rest[-1]
    for slot, blocks in enumerate((own, mate)):
        at_level = level if blocks.shape[0] == levels else 0
        for row in range(rows):
            at = (((slot * 2 + which) * levels + level) * rows + row) * per_row
            left = jnp.concatenate([blocks[at_level, row, k] for k in range(per_row)], axis=1)
            right = jnp.concatenate(
                [stored[numbers[at + k] - base] for k in range(per_row)], axis=0
            )
            out[row, slot] = jnp.dot(left, right, preferred_element_type=F32).astype(BF16)


def row_sums(level, base, which, numbers, own, mate, stored, others=()):
    _, rows, per_row, width, _ = own.shape
    vmem = pl.BlockSpec(memory_space=pltpu.VMEM)
    return pl.pallas_call(
        functools.partial(rows_kernel, level, base, which),
        grid_spec=pltpu.PrefetchScalarGridSpec(
            num_scalar_prefetch=1,
            grid=(1,),
            in_specs=[vmem] * (3 + len(others)),
            out_specs=vmem,
        ),
        out_shape=jax.ShapeDtypeStruct((rows, 2, width, stored.shape[2]), BF16),
        compiler_params=pltpu.CompilerParams(vmem_limit_bytes=8 << 20),
    )(numbers, own, mate, stored, *others)


def shards(
    n_prow,
    right_side,
    lower_inverse,
    upper_inverse,
    lower_blocks,
    lower_index,
    upper_blocks,
    upper_index,
):
    levels, _, width, columns = right_side.shape
    half = columns // 2
    core = lax.rem(lax.axis_index("prow"), 2).astype(jnp.int32)
    core_ref = core.reshape(1)
    mates = [(i, i ^ 1) for i in range(n_prow)]
    planes = [[i * 2 + c for i in range(n_prow // 2)] for c in range(2)]
    copies = n_prow // 2
    n_pcol = lax.axis_size("pcol")
    behind = [
        (i * n_pcol + k, i * n_pcol + (k + 3) % n_pcol)
        for i in range(1, n_prow, 2)
        for k in range(n_pcol)
    ]

    def swap(x):
        return lax.ppermute(x, "prow", mates)

    index = [lower_index, upper_index]
    index = jnp.stack(index + [swap(x) for x in index])
    mine, given, near = first_call(
        core_ref, right_side, lower_inverse, upper_inverse, lower_blocks
    )
    got = swap(given)
    numbers = jnp.bitwise_xor(index, core).reshape(-1)
    lower_given, upper_given, _, _ = lax.optimization_barrier(
        (lower_blocks, upper_blocks, got, numbers)
    )
    lower_mate, upper_mate = swap(lower_given), swap(upper_given)

    token = mine
    for _ in range(1):
        token = lax.ppermute(token, ("prow", "pcol"), behind)

    def heard(sent):
        got = lax.all_to_all(sent, "prow", 0, 0, axis_index_groups=planes)
        return got.reshape(n_prow, width, half)

    def collect(x):
        return lax.all_to_all(x, "pcol", 0, 0)

    sent = spread_call(copies, mine, got, [numbers, token])
    low, pieces = [()], [heard(sent)]
    for height in range(1, levels):
        sums = row_sums(
            height - 1,
            0,
            0,
            numbers,
            near if height == 1 else lower_blocks,
            lower_mate,
            jnp.concatenate(pieces),
            [upper_mate] if height == 2 else [],
        )
        turn = height == levels - 1
        picks = [height, levels + height] if turn else [height]
        x, sent = solve_call(2 * levels + height, picks, copies, collect(sums), mine, got)
        if not turn:
            low.append((x,))
            pieces.append(heard(sent))
    solved, pieces = {levels - 1: x}, []
    for height in range(levels - 2, -1, -1):
        pieces.insert(0, heard(sent))
        sums = row_sums(
            height,
            (height + 1) * n_prow,
            1,
            numbers,
            upper_blocks,
            upper_mate,
            jnp.concatenate(pieces),
        )
        x, *sent = solve_call(
            3 * levels,
            [levels + height],
            copies if height else 0,
            collect(sums),
            mine,
            got,
            low[height],
        )
        sent = sent[0] if sent else None
        solved[height] = x
    pairs = jnp.stack([solved[h] for h in range(levels)])
    kept, came = pairs[:, 0], swap(pairs[:, 1])
    first = jnp.where(core == 0, kept, came)
    second = jnp.where(core == 0, came, kept)
    return jnp.concatenate([first, second], axis=2)[:, None]


def solution(mesh):
    placed = (
        P(None, ("prow", "pcol"), None, None),
        P(None, ("prow", "pcol"), None, None),
        P(None, ("prow", "pcol"), None, None),
        P(None, "prow", "pcol", None, None),
        P(None, "prow", "pcol"),
        P(None, "prow", "pcol", None, None),
        P(None, "prow", "pcol"),
    )
    return jax.shard_map(
        functools.partial(shards, mesh.shape["prow"]),
        mesh=mesh,
        in_specs=placed,
        out_specs=P(None, ("prow", "pcol"), None, None),
        check_vma=False,
    )
```

time: 300 us -> 298 us (level)
  blocking collectives: 241 us -> 246 us
  starting transfers between devices: 13.7 us -> 9.03 us
    ppermute x5 -> x1, starting transfers between devices: 9.54 us -> 4.5 us  [shards(): token = lax.ppermute(token, ('prow', 'pcol'), behind)]
    ppermute x5 -> x1, waiting for transfers between devices: 19.6 us -> 19.4 us  [shards(): token = lax.ppermute(token, ('prow', 'pcol'), behind)]
  transfers between devices with their start and end apart: 10 -> 7, of which waited for: 7 -> 3; matrix products, arithmetic and copies ran while one was open for 0% -> 0% of each run, Pallas kernels for 1% -> 1%
where the time goes in v4:
time: 298 us; the launch traced here: 297 us
  blocking collectives  246 us (83%)
  waiting for transfers between devices  21.8 us (7%)
  Pallas kernels  16.8 us (6%)
  starting transfers between devices  9.03 us (3%)
  other arithmetic  3 us (1%)
    all_to_all x8, blocking collectives, collect(): return lax.all_to_all(x, 'pcol', 0, 0)  124 us
    all_to_all x8, blocking collectives, heard(): got = lax.all_to_all(sent, 'prow', 0, 0, axis_index_groups=planes)  122 us
    ppermute x1, waiting for transfers between devices, shards(): token = lax.ppermute(token, ('prow', 'pcol'), behind)  19.4 us
    pallas_call x8, Pallas kernels, row_sums(): pl.pallas_call(functools.partial(rows_kernel, level, base, which), grid_s...  12.5 us
  transfers between devices with their start and end apart: 7, of which 3 were waited for; matrix products, arithmetic and copies ran while one was open for 0% of the time, Pallas kernels for 1%

profile of v4, /device:TPU:1, one launch (start us, length us, event | category | flops | bytes accessed | tf_op | source)
XLA Modules:
  0.0 297.2 jit_solution(12932877627822169531)
XLA Ops:
  0.0 1.7 shard_map.73
  1.7 3.3 %collective-permute-start.2 = (bf16[16,128,128]{2,1,0:T(8,128)(2,1)S(1)}, bf16[16,128,128]{2,1,0:T(8,128)(2,1)S(1)}, u32[]{:S(2)}, u32[]{:S(2)}) collective-permute-start(bf16[16,128,128]{2,1,0:T(8,128)(2,1)S(1)} %get-tuple-element.24), channel_id=1, source_target_pairs={{0,8},{8,0},{16,24},{24,16},{32,40},{40,32},{48,56},{56,48},{64,72... | collective-permute-start | bytes 1572872 | tf_op jit(solution)/shard_map/ppermute | solution.py:176
  7.5 4.5 %collective-permute-start.5 = (bf16[16,128,128]{2,1,0:T(8,128)(2,1)S(1)}, bf16[16,128,128]{2,1,0:T(8,128)(2,1)S(1)}, u32[]{:S(2)}, u32[]{:S(2)}) collective-permute-start(bf16[16,128,128]{2,1,0:T(8,128)(2,1)S(1)} %get-tuple-element.27.mine), channel_id=1, source_target_pairs={{8,11},{9,12},{10,13},{11,14},{12,15},{13,8},{14,9},{15,10},{24,27... | collective-permute-start | bytes 1572872 | tf_op jit(solution)/shard_map/ppermute | solution.py:192
  12.0 19.4 %collective-permute-done.5.rest_1_ = bf16[16,128,128]{2,1,0:T(8,128)(2,1)S(1)} collective-permute-done((bf16[16,128,128]{2,1,0:T(8,128)(2,1)S(1)}, bf16[16,128,128]{2,1,0:T(8,128)(2,1)S(1)}, u32[]{:S(2)}, u32[]{:S(2)}) %collective-permute-start.5) | collective-permute-done | bytes 524320 | tf_op jit(solution)/shard_map/ppermute | solution.py:192
  31.6 18.7 %all_to_all.80 = bf16[16,2,128,128]{3,2,1,0:T(8,128)(2,1)S(1)} all-to-all(bf16[16,2,128,128]{3,2,1,0:T(8,128)(2,1)S(1)} %shard_map.74), channel_id=1, replica_groups={{0,16,32,48,64,80,96,112,128,144,160,176,192,208,224,240},{8,24,40,56,7..., dimensions={0} | all-to-all | bytes 2097152 | tf_op jit(solution)/shard_map/all_to_all | solution.py:195
  50.3 1.6 shard_map.75
  51.8 17.7 %all_to_all.81.terms = bf16[8,2,128,128]{3,2,1,0:T(8,128)(2,1)S(1)} all-to-all(bf16[8,2,128,128]{3,2,1,0:T(8,128)(2,1)S(1)} %shard_map.75), channel_id=1, replica_groups=mesh['prow'=32,'pcol'=8] {'pcol'}, dimensions={0} | all-to-all | bytes 1048576 | tf_op jit(solution)/shard_map/all_to_all | solution.py:199
  69.9 14.5 %all_to_all.82 = bf16[16,2,128,128]{3,2,1,0:T(8,128)(2,1)S(1)} all-to-all(bf16[16,2,128,128]{3,2,1,0:T(8,128)(2,1)S(1)} %get-tuple-element.29), channel_id=1, replica_groups={{0,16,32,48,64,80,96,112,128,144,160,176,192,208,224,240},{8,24,40,56,7..., dimensions={0} | all-to-all | bytes 2097152 | tf_op jit(solution)/shard_map/all_to_all | solution.py:195
  86.2 14.5 %all_to_all.83.terms = bf16[8,2,128,128]{3,2,1,0:T(8,128)(2,1)S(1)} all-to-all(bf16[8,2,128,128]{3,2,1,0:T(8,128)(2,1)S(1)} %shard_map.77), channel_id=1, replica_groups=mesh['prow'=32,'pcol'=8] {'pcol'}, dimensions={0} | all-to-all | bytes 1048576 | tf_op jit(solution)/shard_map/all_to_all | solution.py:199
  101.0 14.5 %all_to_all.84 = bf16[16,2,128,128]{3,2,1,0:T(8,128)(2,1)S(1)} all-to-all(bf16[16,2,128,128]{3,2,1,0:T(8,128)(2,1)S(1)} %get-tuple-element.30), channel_id=1, replica_groups={{0,16,32,48,64,80,96,112,128,144,160,176,192,208,224,240},{8,24,40,56,7..., dimensions={0} | all-to-all | bytes 2097152 | tf_op jit(solution)/shard_map/all_to_all | solution.py:195
  117.4 14.8 %all_to_all.85.terms = bf16[8,2,128,128]{3,2,1,0:T(8,128)(2,1)S(1)} all-to-all(bf16[8,2,128,128]{3,2,1,0:T(8,128)(2,1)S(1)} %shard_map.79), channel_id=1, replica_groups=mesh['prow'=32,'pcol'=8] {'pcol'}, dimensions={0} | all-to-all | bytes 1048576 | tf_op jit(solution)/shard_map/all_to_all | solution.py:199
  132.6 14.5 %all_to_all.86 = bf16[16,2,128,128]{3,2,1,0:T(8,128)(2,1)S(1)} all-to-all(bf16[16,2,128,128]{3,2,1,0:T(8,128)(2,1)S(1)} %get-tuple-element.31), channel_id=1, replica_groups={{0,16,32,48,64,80,96,112,128,144,160,176,192,208,224,240},{8,24,40,56,7..., dimensions={0} | all-to-all | bytes 2097152 | tf_op jit(solution)/shard_map/all_to_all | solution.py:195
  149.2 14.6 %all_to_all.87.terms = bf16[8,2,128,128]{3,2,1,0:T(8,128)(2,1)S(1)} all-to-all(bf16[8,2,128,128]{3,2,1,0:T(8,128)(2,1)S(1)} %shard_map.81), channel_id=1, replica_groups=mesh['prow'=32,'pcol'=8] {'pcol'}, dimensions={0} | all-to-all | bytes 1048576 | tf_op jit(solution)/shard_map/all_to_all | solution.py:199
  164.2 14.5 %all_to_all.88 = bf16[16,2,128,128]{3,2,1,0:T(8,128)(2,1)S(1)} all-to-all(bf16[16,2,128,128]{3,2,1,0:T(8,128)(2,1)S(1)} %get-tuple-element.32), channel_id=1, replica_groups={{0,16,32,48,64,80,96,112,128,144,160,176,192,208,224,240},{8,24,40,56,7..., dimensions={0} | all-to-all | bytes 2097152 | tf_op jit(solution)/shard_map/all_to_all | solution.py:195
  178.7 1.6 shard_map.83
  180.3 14.5 %all_to_all.89.terms = bf16[8,2,128,128]{3,2,1,0:T(8,128)(2,1)S(1)} all-to-all(bf16[8,2,128,128]{3,2,1,0:T(8,128)(2,1)S(1)} %shard_map.83), channel_id=1, replica_groups=mesh['prow'=32,'pcol'=8] {'pcol'}, dimensions={0} | all-to-all | bytes 1048576 | tf_op jit(solution)/shard_map/all_to_all | solution.py:199
  195.1 14.6 %all_to_all.90 = bf16[16,2,128,128]{3,2,1,0:T(8,128)(2,1)S(1)} all-to-all(bf16[16,2,128,128]{3,2,1,0:T(8,128)(2,1)S(1)} %get-tuple-element.34), channel_id=1, replica_groups={{0,16,32,48,64,80,96,112,128,144,160,176,192,208,224,240},{8,24,40,56,7..., dimensions={0} | all-to-all | bytes 2097152 | tf_op jit(solution)/shard_map/all_to_all | solution.py:195
  210.0 1.6 shard_map.85
  211.5 14.5 %all_to_all.91.terms = bf16[8,2,128,128]{3,2,1,0:T(8,128)(2,1)S(1)} all-to-all(bf16[8,2,128,128]{3,2,1,0:T(8,128)(2,1)S(1)} %shard_map.85), channel_id=1, replica_groups=mesh['prow'=32,'pcol'=8] {'pcol'}, dimensions={0} | all-to-all | bytes 1048576 | tf_op jit(solution)/shard_map/all_to_all | solution.py:199
  226.4 14.5 %all_to_all.92 = bf16[16,2,128,128]{3,2,1,0:T(8,128)(2,1)S(1)} all-to-all(bf16[16,2,128,128]{3,2,1,0:T(8,128)(2,1)S(1)} %get-tuple-element.36), channel_id=1, replica_groups={{0,16,32,48,64,80,96,112,128,144,160,176,192,208,224,240},{8,24,40,56,7..., dimensions={0} | all-to-all | bytes 2097152 | tf_op jit(solution)/shard_map/all_to_all | solution.py:195
  242.8 15.3 %all_to_all.93.terms = bf16[8,2,128,128]{3,2,1,0:T(8,128)(2,1)S(1)} all-to-all(bf16[8,2,128,128]{3,2,1,0:T(8,128)(2,1)S(1)} %shard_map.87), channel_id=1, replica_groups=mesh['prow'=32,'pcol'=8] {'pcol'}, dimensions={0} | all-to-all | bytes 1048576 | tf_op jit(solution)/shard_map/all_to_all | solution.py:199
  258.4 16.4 %all_to_all.94 = bf16[16,2,128,128]{3,2,1,0:T(8,128)(2,1)S(1)} all-to-all(bf16[16,2,128,128]{3,2,1,0:T(8,128)(2,1)S(1)} %get-tuple-element.38), channel_id=1, replica_groups={{0,16,32,48,64,80,96,112,128,144,160,176,192,208,224,240},{8,24,40,56,7..., dimensions={0} | all-to-all | bytes 2097152 | tf_op jit(solution)/shard_map/all_to_all | solution.py:195
  275.4 1.6 shard_map.89
  276.9 17.6 %all_to_all.95.terms = bf16[8,2,128,128]{3,2,1,0:T(8,128)(2,1)S(1)} all-to-all(bf16[8,2,128,128]{3,2,1,0:T(8,128)(2,1)S(1)} %shard_map.89), channel_id=1, replica_groups=mesh['prow'=32,'pcol'=8] {'pcol'}, dimensions={0} | all-to-all | bytes 1048576 | tf_op jit(solution)/shard_map/all_to_all | solution.py:199
  (55 shorter events, 15.8 us)
Async XLA Ops:
  0.0 5.0 %copy-start.1 = (s32[4,8,6]{1,0,2:T(4,128)S(1)}, s32[4,8,6]{1,0,2:T(4,128)}, u32[]{:S(2)}) copy-start(s32[4,8,6]{1,0,2:T(4,128)} %param.11) | copy-start | bytes 2308
  0.0 5.1 %copy-start = (s32[4,8,6]{1,0,2:T(4,128)S(1)}, s32[4,8,6]{1,0,2:T(4,128)}, u32[]{:S(2)}) copy-start(s32[4,8,6]{1,0,2:T(4,128)} %param.13) | copy-start | bytes 2308
  1.7 5.2 %collective-permute-start.2 = (bf16[16,128,128]{2,1,0:T(8,128)(2,1)S(1)}, bf16[16,128,128]{2,1,0:T(8,128)(2,1)S(1)}, u32[]{:S(2)}, u32[]{:S(2)}) collective-permute-start(bf16[16,128,128]{2,1,0:T(8,128)(2,1)S(1)} %get-tuple-element.24), channel_id=1, source_target_pairs={{0,8},{8,0},{16,24},{24,16},{32,40},{40,32},{48,56},{56,48},{64,72... | collective-permute-start | bytes 1572872 | tf_op jit(solution)/shard_map/ppermute | solution.py:176
  5.0 1.6 collective-permute-start
  5.1 1.5 collective-permute-start.1
  6.9 43.3 %collective-permute-start.4 = (bf16[4,8,6,128,128]{4,3,2,1,0:T(8,128)(2,1)}, bf16[4,8,6,128,128]{4,3,2,1,0:T(8,128)(2,1)S(1)}, u32[]{:S(2)}, u32[]{:S(2)}) collective-permute-start(bf16[4,8,6,128,128]{4,3,2,1,0:T(8,128)(2,1)} %own.9), channel_id=1, source_target_pairs={{0,8},{8,0},{16,24},{24,16},{32,40},{40,32},{48,56},{56,48},{64,72... | collective-permute-start | bytes 18874376 | tf_op jit(solution)/shard_map/ppermute | solution.py:176
  7.4 77.2 %collective-permute-start.3 = (bf16[4,8,6,128,128]{4,3,2,1,0:T(8,128)(2,1)}, bf16[4,8,6,128,128]{4,3,2,1,0:T(8,128)(2,1)S(1)}, u32[]{:S(2)}, u32[]{:S(2)}) collective-permute-start(bf16[4,8,6,128,128]{4,3,2,1,0:T(8,128)(2,1)} %own.13), channel_id=1, source_target_pairs={{0,8},{8,0},{16,24},{24,16},{32,40},{40,32},{48,56},{56,48},{64,72... | collective-permute-start | bytes 18874376 | tf_op jit(solution)/shard_map/ppermute | solution.py:176
  7.5 23.9 %collective-permute-start.5 = (bf16[16,128,128]{2,1,0:T(8,128)(2,1)S(1)}, bf16[16,128,128]{2,1,0:T(8,128)(2,1)S(1)}, u32[]{:S(2)}, u32[]{:S(2)}) collective-permute-start(bf16[16,128,128]{2,1,0:T(8,128)(2,1)S(1)} %get-tuple-element.27.mine), channel_id=1, source_target_pairs={{8,11},{9,12},{10,13},{11,14},{12,15},{13,8},{14,9},{15,10},{24,27... | collective-permute-start | bytes 1572872 | tf_op jit(solution)/shard_map/ppermute | solution.py:192
  31.6 53.0 %slice-start.2 = ((s8[6291456]{0:T(1024)(128)(4,1)}), s8[4194304]{0:T(1024)(128)(4,1)S(1)}, s32[]{:S(2)}) async-start(s8[6291456]{0:T(1024)(128)(4,1)} %bitcast.41), calls=%async_computation.18 | async-start | bytes 8388608
  50.3 34.3 %slice-start.3 = ((s8[6291456]{0:T(1024)(128)(4,1)}), s8[2097152]{0:T(1024)(128)(4,1)S(1)}, s32[]{:S(2)}) async-start(s8[6291456]{0:T(1024)(128)(4,1)} %bitcast.41), calls=%async_computation.19 | async-start | bytes 4194304
  147.0 31.6 %slice-start = ((s8[6291456]{0:T(1024)(128)(4,1)}), s8[4194304]{0:T(1024)(128)(4,1)S(1)}, s32[]{:S(2)}) async-start(s8[6291456]{0:T(1024)(128)(4,1)} %bitcast.39), calls=%async_computation.16 | async-start | bytes 8388608
  147.6 31.1 %slice-start.1 = ((s8[6291456]{0:T(1024)(128)(4,1)}), s8[2097152]{0:T(1024)(128)(4,1)S(1)}, s32[]{:S(2)}) async-start(s8[6291456]{0:T(1024)(128)(4,1)} %bitcast.39), calls=%async_computation.17 | async-start | bytes 4194304
  294.9 1.5 collective-permute-start.6

commit v5 on v4

--- a/solution.py
+++ b/solution.py
@@ -38,13 +38,15 @@
         out[3 * levels] = jnp.dot(
             lowers[0, 0], sides[0, 0, :, part], preferred_element_type=F32
         ).astype(BF16)
+        out[3 * levels + 1] = out[3 * levels]
+        out[3 * levels + 2] = out[3 * levels]
     for i in range(3, 5):
         copy(i).wait()
 
 
 def first_call(core, *arrays):
     levels, _, width, columns = arrays[0].shape
-    packed = jax.ShapeDtypeStruct((3 * levels + 1, width, columns // 2), BF16)
+    packed = jax.ShapeDtypeStruct((3 * levels + 3, width, columns // 2), BF16)
     near = jax.ShapeDtypeStruct((1,) + arrays[3].shape[1:], BF16)
     arrays = [pltpu.with_memory_space_constraint(x, pltpu.HBM) for x in arrays]
     return pl.pallas_call(

time: 298 us -> 296 us (level)
  blocking collectives: 246 us -> 243 us
where the time goes in v5:
time: 296 us; the launch traced here: 295 us
  blocking collectives  243 us (82%)
  waiting for transfers between devices  22.6 us (8%)
  Pallas kernels  16.8 us (6%)
  starting transfers between devices  9.03 us (3%)
  other arithmetic  3 us (1%)
    all_to_all x8, blocking collectives, collect(): return lax.all_to_all(x, 'pcol', 0, 0)  123 us
    all_to_all x8, blocking collectives, heard(): got = lax.all_to_all(sent, 'prow', 0, 0, axis_index_groups=planes)  120 us
    ppermute x1, waiting for transfers between devices, shards(): token = lax.ppermute(token, ('prow', 'pcol'), behind)  20.1 us
    pallas_call x8, Pallas kernels, row_sums(): pl.pallas_call(functools.partial(rows_kernel, level, base, which), grid_s...  12.5 us
  transfers between devices with their start and end apart: 7, of which 3 were waited for; matrix products, arithmetic and copies ran while one was open for 0% of the time, Pallas kernels for 1%

profile of v5, /device:TPU:1, one launch (start us, length us, event | category | flops | bytes accessed | tf_op | source)
XLA Modules:
  0.0 295.3 jit_solution(4341596822829891829)
XLA Ops:
  0.0 1.7 shard_map.73
  1.7 3.3 %collective-permute-start.2 = (bf16[18,128,128]{2,1,0:T(8,128)(2,1)S(1)}, bf16[18,128,128]{2,1,0:T(8,128)(2,1)S(1)}, u32[]{:S(2)}, u32[]{:S(2)}) collective-permute-start(bf16[18,128,128]{2,1,0:T(8,128)(2,1)S(1)} %get-tuple-element.24), channel_id=1, source_target_pairs={{0,8},{8,0},{16,24},{24,16},{32,40},{40,32},{48,56},{56,48},{64,72... | collective-permute-start | bytes 1769480 | tf_op jit(solution)/shard_map/ppermute | solution.py:178
  7.6 4.5 %collective-permute-start.5 = (bf16[18,128,128]{2,1,0:T(8,128)(2,1)S(1)}, bf16[18,128,128]{2,1,0:T(8,128)(2,1)S(1)}, u32[]{:S(2)}, u32[]{:S(2)}) collective-permute-start(bf16[18,128,128]{2,1,0:T(8,128)(2,1)S(1)} %get-tuple-element.27.mine), channel_id=1, source_target_pairs={{8,11},{9,12},{10,13},{11,14},{12,15},{13,8},{14,9},{15,10},{24,27... | collective-permute-start | bytes 1769480 | tf_op jit(solution)/shard_map/ppermute | solution.py:194
  12.1 20.1 %collective-permute-done.5.rest_1_ = bf16[18,128,128]{2,1,0:T(8,128)(2,1)S(1)} collective-permute-done((bf16[18,128,128]{2,1,0:T(8,128)(2,1)S(1)}, bf16[18,128,128]{2,1,0:T(8,128)(2,1)S(1)}, u32[]{:S(2)}, u32[]{:S(2)}) %collective-permute-start.5) | collective-permute-done | bytes 589856 | tf_op jit(solution)/shard_map/ppermute | solution.py:194
  32.4 18.7 %all_to_all.80 = bf16[16,2,128,128]{3,2,1,0:T(8,128)(2,1)S(1)} all-to-all(bf16[16,2,128,128]{3,2,1,0:T(8,128)(2,1)S(1)} %shard_map.74), channel_id=1, replica_groups={{0,16,32,48,64,80,96,112,128,144,160,176,192,208,224,240},{8,24,40,56,7..., dimensions={0} | all-to-all | bytes 2097152 | tf_op jit(solution)/shard_map/all_to_all | solution.py:197
  51.1 1.6 shard_map.75
  52.6 19.1 %all_to_all.81.terms = bf16[8,2,128,128]{3,2,1,0:T(8,128)(2,1)S(1)} all-to-all(bf16[8,2,128,128]{3,2,1,0:T(8,128)(2,1)S(1)} %shard_map.75), channel_id=1, replica_groups=mesh['prow'=32,'pcol'=8] {'pcol'}, dimensions={0} | all-to-all | bytes 1048576 | tf_op jit(solution)/shard_map/all_to_all | solution.py:201
  72.1 14.5 %all_to_all.82 = bf16[16,2,128,128]{3,2,1,0:T(8,128)(2,1)S(1)} all-to-all(bf16[16,2,128,128]{3,2,1,0:T(8,128)(2,1)S(1)} %get-tuple-element.29), channel_id=1, replica_groups={{0,16,32,48,64,80,96,112,128,144,160,176,192,208,224,240},{8,24,40,56,7..., dimensions={0} | all-to-all | bytes 2097152 | tf_op jit(solution)/shard_map/all_to_all | solution.py:197
  88.4 14.5 %all_to_all.83.terms = bf16[8,2,128,128]{3,2,1,0:T(8,128)(2,1)S(1)} all-to-all(bf16[8,2,128,128]{3,2,1,0:T(8,128)(2,1)S(1)} %shard_map.77), channel_id=1, replica_groups=mesh['prow'=32,'pcol'=8] {'pcol'}, dimensions={0} | all-to-all | bytes 1048576 | tf_op jit(solution)/shard_map/all_to_all | solution.py:201
  103.2 14.5 %all_to_all.84 = bf16[16,2,128,128]{3,2,1,0:T(8,128)(2,1)S(1)} all-to-all(bf16[16,2,128,128]{3,2,1,0:T(8,128)(2,1)S(1)} %get-tuple-element.30), channel_id=1, replica_groups={{0,16,32,48,64,80,96,112,128,144,160,176,192,208,224,240},{8,24,40,56,7..., dimensions={0} | all-to-all | bytes 2097152 | tf_op jit(solution)/shard_map/all_to_all | solution.py:197
  119.6 14.5 %all_to_all.85.terms = bf16[8,2,128,128]{3,2,1,0:T(8,128)(2,1)S(1)} all-to-all(bf16[8,2,128,128]{3,2,1,0:T(8,128)(2,1)S(1)} %shard_map.79), channel_id=1, replica_groups=mesh['prow'=32,'pcol'=8] {'pcol'}, dimensions={0} | all-to-all | bytes 1048576 | tf_op jit(solution)/shard_map/all_to_all | solution.py:201
  134.5 14.5 %all_to_all.86 = bf16[16,2,128,128]{3,2,1,0:T(8,128)(2,1)S(1)} all-to-all(bf16[16,2,128,128]{3,2,1,0:T(8,128)(2,1)S(1)} %get-tuple-element.31), channel_id=1, replica_groups={{0,16,32,48,64,80,96,112,128,144,160,176,192,208,224,240},{8,24,40,56,7..., dimensions={0} | all-to-all | bytes 2097152 | tf_op jit(solution)/shard_map/all_to_all | solution.py:197
  151.1 14.8 %all_to_all.87.terms = bf16[8,2,128,128]{3,2,1,0:T(8,128)(2,1)S(1)} all-to-all(bf16[8,2,128,128]{3,2,1,0:T(8,128)(2,1)S(1)} %shard_map.81), channel_id=1, replica_groups=mesh['prow'=32,'pcol'=8] {'pcol'}, dimensions={0} | all-to-all | bytes 1048576 | tf_op jit(solution)/shard_map/all_to_all | solution.py:201
  166.3 14.5 %all_to_all.88 = bf16[16,2,128,128]{3,2,1,0:T(8,128)(2,1)S(1)} all-to-all(bf16[16,2,128,128]{3,2,1,0:T(8,128)(2,1)S(1)} %get-tuple-element.32), channel_id=1, replica_groups={{0,16,32,48,64,80,96,112,128,144,160,176,192,208,224,240},{8,24,40,56,7..., dimensions={0} | all-to-all | bytes 2097152 | tf_op jit(solution)/shard_map/all_to_all | solution.py:197
  180.8 1.6 shard_map.83
  182.4 14.8 %all_to_all.89.terms = bf16[8,2,128,128]{3,2,1,0:T(8,128)(2,1)S(1)} all-to-all(bf16[8,2,128,128]{3,2,1,0:T(8,128)(2,1)S(1)} %shard_map.83), channel_id=1, replica_groups=mesh['prow'=32,'pcol'=8] {'pcol'}, dimensions={0} | all-to-all | bytes 1048576 | tf_op jit(solution)/shard_map/all_to_all | solution.py:201
  197.6 14.6 %all_to_all.90 = bf16[16,2,128,128]{3,2,1,0:T(8,128)(2,1)S(1)} all-to-all(bf16[16,2,128,128]{3,2,1,0:T(8,128)(2,1)S(1)} %get-tuple-element.34), channel_id=1, replica_groups={{0,16,32,48,64,80,96,112,128,144,160,176,192,208,224,240},{8,24,40,56,7..., dimensions={0} | all-to-all | bytes 2097152 | tf_op jit(solution)/shard_map/all_to_all | solution.py:197
  212.4 1.6 shard_map.85
  213.9 14.5 %all_to_all.91.terms = bf16[8,2,128,128]{3,2,1,0:T(8,128)(2,1)S(1)} all-to-all(bf16[8,2,128,128]{3,2,1,0:T(8,128)(2,1)S(1)} %shard_map.85), channel_id=1, replica_groups=mesh['prow'=32,'pcol'=8] {'pcol'}, dimensions={0} | all-to-all | bytes 1048576 | tf_op jit(solution)/shard_map/all_to_all | solution.py:201
  228.8 14.5 %all_to_all.92 = bf16[16,2,128,128]{3,2,1,0:T(8,128)(2,1)S(1)} all-to-all(bf16[16,2,128,128]{3,2,1,0:T(8,128)(2,1)S(1)} %get-tuple-element.36), channel_id=1, replica_groups={{0,16,32,48,64,80,96,112,128,144,160,176,192,208,224,240},{8,24,40,56,7..., dimensions={0} | all-to-all | bytes 2097152 | tf_op jit(solution)/shard_map/all_to_all | solution.py:197
  245.2 14.5 %all_to_all.93.terms = bf16[8,2,128,128]{3,2,1,0:T(8,128)(2,1)S(1)} all-to-all(bf16[8,2,128,128]{3,2,1,0:T(8,128)(2,1)S(1)} %shard_map.87), channel_id=1, replica_groups=mesh['prow'=32,'pcol'=8] {'pcol'}, dimensions={0} | all-to-all | bytes 1048576 | tf_op jit(solution)/shard_map/all_to_all | solution.py:201
  260.1 14.4 %all_to_all.94 = bf16[16,2,128,128]{3,2,1,0:T(8,128)(2,1)S(1)} all-to-all(bf16[16,2,128,128]{3,2,1,0:T(8,128)(2,1)S(1)} %get-tuple-element.38), channel_id=1, replica_groups={{0,16,32,48,64,80,96,112,128,144,160,176,192,208,224,240},{8,24,40,56,7..., dimensions={0} | all-to-all | bytes 2097152 | tf_op jit(solution)/shard_map/all_to_all | solution.py:197
  275.1 1.6 shard_map.89
  276.6 16.1 %all_to_all.95.terms = bf16[8,2,128,128]{3,2,1,0:T(8,128)(2,1)S(1)} all-to-all(bf16[8,2,128,128]{3,2,1,0:T(8,128)(2,1)S(1)} %shard_map.89), channel_id=1, replica_groups=mesh['prow'=32,'pcol'=8] {'pcol'}, dimensions={0} | all-to-all | bytes 1048576 | tf_op jit(solution)/shard_map/all_to_all | solution.py:201
  (55 shorter events, 15.9 us)
Async XLA Ops:
  0.0 5.0 %copy-start.1 = (s32[4,8,6]{1,0,2:T(4,128)S(1)}, s32[4,8,6]{1,0,2:T(4,128)}, u32[]{:S(2)}) copy-start(s32[4,8,6]{1,0,2:T(4,128)} %param.11) | copy-start | bytes 2308
  0.0 5.1 %copy-start = (s32[4,8,6]{1,0,2:T(4,128)S(1)}, s32[4,8,6]{1,0,2:T(4,128)}, u32[]{:S(2)}) copy-start(s32[4,8,6]{1,0,2:T(4,128)} %param.13) | copy-start | bytes 2308
  1.7 5.3 %collective-permute-start.2 = (bf16[18,128,128]{2,1,0:T(8,128)(2,1)S(1)}, bf16[18,128,128]{2,1,0:T(8,128)(2,1)S(1)}, u32[]{:S(2)}, u32[]{:S(2)}) collective-permute-start(bf16[18,128,128]{2,1,0:T(8,128)(2,1)S(1)} %get-tuple-element.24), channel_id=1, source_target_pairs={{0,8},{8,0},{16,24},{24,16},{32,40},{40,32},{48,56},{56,48},{64,72... | collective-permute-start | bytes 1769480 | tf_op jit(solution)/shard_map/ppermute | solution.py:178
  5.0 1.6 collective-permute-start
  5.1 1.6 collective-permute-start.1
  7.0 44.0 %collective-permute-start.4 = (bf16[4,8,6,128,128]{4,3,2,1,0:T(8,128)(2,1)}, bf16[4,8,6,128,128]{4,3,2,1,0:T(8,128)(2,1)S(1)}, u32[]{:S(2)}, u32[]{:S(2)}) collective-permute-start(bf16[4,8,6,128,128]{4,3,2,1,0:T(8,128)(2,1)} %own.9), channel_id=1, source_target_pairs={{0,8},{8,0},{16,24},{24,16},{32,40},{40,32},{48,56},{56,48},{64,72... | collective-permute-start | bytes 18874376 | tf_op jit(solution)/shard_map/ppermute | solution.py:178
  7.5 79.3 %collective-permute-start.3 = (bf16[4,8,6,128,128]{4,3,2,1,0:T(8,128)(2,1)}, bf16[4,8,6,128,128]{4,3,2,1,0:T(8,128)(2,1)S(1)}, u32[]{:S(2)}, u32[]{:S(2)}) collective-permute-start(bf16[4,8,6,128,128]{4,3,2,1,0:T(8,128)(2,1)} %own.13), channel_id=1, source_target_pairs={{0,8},{8,0},{16,24},{24,16},{32,40},{40,32},{48,56},{56,48},{64,72... | collective-permute-start | bytes 18874376 | tf_op jit(solution)/shard_map/ppermute | solution.py:178
  7.6 24.6 %collective-permute-start.5 = (bf16[18,128,128]{2,1,0:T(8,128)(2,1)S(1)}, bf16[18,128,128]{2,1,0:T(8,128)(2,1)S(1)}, u32[]{:S(2)}, u32[]{:S(2)}) collective-permute-start(bf16[18,128,128]{2,1,0:T(8,128)(2,1)S(1)} %get-tuple-element.27.mine), channel_id=1, source_target_pairs={{8,11},{9,12},{10,13},{11,14},{12,15},{13,8},{14,9},{15,10},{24,27... | collective-permute-start | bytes 1769480 | tf_op jit(solution)/shard_map/ppermute | solution.py:194
  32.4 54.4 %slice-start.2 = ((s8[6291456]{0:T(1024)(128)(4,1)}), s8[4194304]{0:T(1024)(128)(4,1)S(1)}, s32[]{:S(2)}) async-start(s8[6291456]{0:T(1024)(128)(4,1)} %bitcast.41), calls=%async_computation.18 | async-start | bytes 8388608
  51.1 35.7 %slice-start.3 = ((s8[6291456]{0:T(1024)(128)(4,1)}), s8[2097152]{0:T(1024)(128)(4,1)S(1)}, s32[]{:S(2)}) async-start(s8[6291456]{0:T(1024)(128)(4,1)} %bitcast.41), calls=%async_computation.19 | async-start | bytes 4194304
  148.9 31.9 %slice-start = ((s8[6291456]{0:T(1024)(128)(4,1)}), s8[4194304]{0:T(1024)(128)(4,1)S(1)}, s32[]{:S(2)}) async-start(s8[6291456]{0:T(1024)(128)(4,1)} %bitcast.39), calls=%async_computation.16 | async-start | bytes 8388608
  149.5 31.3 %slice-start.1 = ((s8[6291456]{0:T(1024)(128)(4,1)}), s8[2097152]{0:T(1024)(128)(4,1)S(1)}, s32[]{:S(2)}) async-start(s8[6291456]{0:T(1024)(128)(4,1)} %bitcast.39), calls=%async_computation.17 | async-start | bytes 4194304
  293.0 1.5 collective-permute-start.6

commit v6 on v4

--- a/solution.py
+++ b/solution.py
@@ -38,6 +38,8 @@
         out[3 * levels] = jnp.dot(
             lowers[0, 0], sides[0, 0, :, part], preferred_element_type=F32
         ).astype(BF16)
+        for row in range(3 * levels + 1, out.shape[0]):
+            out[row] = out[3 * levels]
     for i in range(3, 5):
         copy(i).wait()
 
@@ -45,6 +47,7 @@
 def first_call(core, *arrays):
     levels, _, width, columns = arrays[0].shape
     packed = jax.ShapeDtypeStruct((3 * levels + 1, width, columns // 2), BF16)
+    longer = jax.ShapeDtypeStruct((3 * levels + 3, width, columns // 2), BF16)
     near = jax.ShapeDtypeStruct((1,) + arrays[3].shape[1:], BF16)
     arrays = [pltpu.with_memory_space_constraint(x, pltpu.HBM) for x in arrays]
     return pl.pallas_call(
@@ -57,7 +60,7 @@
             scratch_shapes=[pltpu.VMEM(x.shape, BF16) for x in arrays[:3]]
             + [pltpu.SemaphoreType.DMA((5,))],
         ),
-        out_shape=[packed, packed, near],
+        out_shape=[longer, packed, near],
         compiler_params=pltpu.CompilerParams(vmem_limit_bytes=16 << 20),
     )(core, *arrays)
 

time: 298 us -> 296 us (level)
  blocking collectives: 246 us -> 243 us
where the time goes in v6:
time: 296 us; the launch traced here: 295 us
  blocking collectives  243 us (82%)
  waiting for transfers between devices  22.5 us (8%)
  Pallas kernels  16.8 us (6%)
  starting transfers between devices  9.03 us (3%)
  other arithmetic  3 us (1%)
    all_to_all x8, blocking collectives, collect(): return lax.all_to_all(x, 'pcol', 0, 0)  123 us
    all_to_all x8, blocking collectives, heard(): got = lax.all_to_all(sent, 'prow', 0, 0, axis_index_groups=planes)  120 us
    ppermute x1, waiting for transfers between devices, shards(): token = lax.ppermute(token, ('prow', 'pcol'), behind)  20.1 us
    pallas_call x8, Pallas kernels, row_sums(): pl.pallas_call(functools.partial(rows_kernel, level, base, which), grid_s...  12.5 us
  transfers between devices with their start and end apart: 7, of which 3 were waited for; matrix products, arithmetic and copies ran while one was open for 0% of the time, Pallas kernels for 1%

profile of v6, /device:TPU:1, one launch (start us, length us, event | category | flops | bytes accessed | tf_op | source)
XLA Modules:
  0.0 295.2 jit_solution(713273502973735182)
XLA Ops:
  0.0 1.7 shard_map.73
  1.7 3.3 %collective-permute-start.2 = (bf16[16,128,128]{2,1,0:T(8,128)(2,1)S(1)}, bf16[16,128,128]{2,1,0:T(8,128)(2,1)S(1)}, u32[]{:S(2)}, u32[]{:S(2)}) collective-permute-start(bf16[16,128,128]{2,1,0:T(8,128)(2,1)S(1)} %get-tuple-element.24), channel_id=1, source_target_pairs={{0,8},{8,0},{16,24},{24,16},{32,40},{40,32},{48,56},{56,48},{64,72... | collective-permute-start | bytes 1572872 | tf_op jit(solution)/shard_map/ppermute | solution.py:179
  7.5 4.5 %collective-permute-start.5 = (bf16[18,128,128]{2,1,0:T(8,128)(2,1)S(1)}, bf16[18,128,128]{2,1,0:T(8,128)(2,1)S(1)}, u32[]{:S(2)}, u32[]{:S(2)}) collective-permute-start(bf16[18,128,128]{2,1,0:T(8,128)(2,1)S(1)} %get-tuple-element.27.mine), channel_id=1, source_target_pairs={{8,11},{9,12},{10,13},{11,14},{12,15},{13,8},{14,9},{15,10},{24,27... | collective-permute-start | bytes 1769480 | tf_op jit(solution)/shard_map/ppermute | solution.py:195
  12.0 20.1 %collective-permute-done.5.rest_1_ = bf16[18,128,128]{2,1,0:T(8,128)(2,1)S(1)} collective-permute-done((bf16[18,128,128]{2,1,0:T(8,128)(2,1)S(1)}, bf16[18,128,128]{2,1,0:T(8,128)(2,1)S(1)}, u32[]{:S(2)}, u32[]{:S(2)}) %collective-permute-start.5) | collective-permute-done | bytes 589856 | tf_op jit(solution)/shard_map/ppermute | solution.py:195
  32.3 18.7 %all_to_all.80 = bf16[16,2,128,128]{3,2,1,0:T(8,128)(2,1)S(1)} all-to-all(bf16[16,2,128,128]{3,2,1,0:T(8,128)(2,1)S(1)} %shard_map.74), channel_id=1, replica_groups={{0,16,32,48,64,80,96,112,128,144,160,176,192,208,224,240},{8,24,40,56,7..., dimensions={0} | all-to-all | bytes 2097152 | tf_op jit(solution)/shard_map/all_to_all | solution.py:198
  51.0 1.6 shard_map.75
  52.6 19.1 %all_to_all.81.terms = bf16[8,2,128,128]{3,2,1,0:T(8,128)(2,1)S(1)} all-to-all(bf16[8,2,128,128]{3,2,1,0:T(8,128)(2,1)S(1)} %shard_map.75), channel_id=1, replica_groups=mesh['prow'=32,'pcol'=8] {'pcol'}, dimensions={0} | all-to-all | bytes 1048576 | tf_op jit(solution)/shard_map/all_to_all | solution.py:202
  72.0 14.5 %all_to_all.82 = bf16[16,2,128,128]{3,2,1,0:T(8,128)(2,1)S(1)} all-to-all(bf16[16,2,128,128]{3,2,1,0:T(8,128)(2,1)S(1)} %get-tuple-element.29), channel_id=1, replica_groups={{0,16,32,48,64,80,96,112,128,144,160,176,192,208,224,240},{8,24,40,56,7..., dimensions={0} | all-to-all | bytes 2097152 | tf_op jit(solution)/shard_map/all_to_all | solution.py:198
  88.3 14.5 %all_to_all.83.terms = bf16[8,2,128,128]{3,2,1,0:T(8,128)(2,1)S(1)} all-to-all(bf16[8,2,128,128]{3,2,1,0:T(8,128)(2,1)S(1)} %shard_map.77), channel_id=1, replica_groups=mesh['prow'=32,'pcol'=8] {'pcol'}, dimensions={0} | all-to-all | bytes 1048576 | tf_op jit(solution)/shard_map/all_to_all | solution.py:202
  103.1 14.5 %all_to_all.84 = bf16[16,2,128,128]{3,2,1,0:T(8,128)(2,1)S(1)} all-to-all(bf16[16,2,128,128]{3,2,1,0:T(8,128)(2,1)S(1)} %get-tuple-element.30), channel_id=1, replica_groups={{0,16,32,48,64,80,96,112,128,144,160,176,192,208,224,240},{8,24,40,56,7..., dimensions={0} | all-to-all | bytes 2097152 | tf_op jit(solution)/shard_map/all_to_all | solution.py:198
  119.5 14.5 %all_to_all.85.terms = bf16[8,2,128,128]{3,2,1,0:T(8,128)(2,1)S(1)} all-to-all(bf16[8,2,128,128]{3,2,1,0:T(8,128)(2,1)S(1)} %shard_map.79), channel_id=1, replica_groups=mesh['prow'=32,'pcol'=8] {'pcol'}, dimensions={0} | all-to-all | bytes 1048576 | tf_op jit(solution)/shard_map/all_to_all | solution.py:202
  134.4 14.5 %all_to_all.86 = bf16[16,2,128,128]{3,2,1,0:T(8,128)(2,1)S(1)} all-to-all(bf16[16,2,128,128]{3,2,1,0:T(8,128)(2,1)S(1)} %get-tuple-element.31), channel_id=1, replica_groups={{0,16,32,48,64,80,96,112,128,144,160,176,192,208,224,240},{8,24,40,56,7..., dimensions={0} | all-to-all | bytes 2097152 | tf_op jit(solution)/shard_map/all_to_all | solution.py:198
  151.0 14.8 %all_to_all.87.terms = bf16[8,2,128,128]{3,2,1,0:T(8,128)(2,1)S(1)} all-to-all(bf16[8,2,128,128]{3,2,1,0:T(8,128)(2,1)S(1)} %shard_map.81), channel_id=1, replica_groups=mesh['prow'=32,'pcol'=8] {'pcol'}, dimensions={0} | all-to-all | bytes 1048576 | tf_op jit(solution)/shard_map/all_to_all | solution.py:202
  166.2 14.5 %all_to_all.88 = bf16[16,2,128,128]{3,2,1,0:T(8,128)(2,1)S(1)} all-to-all(bf16[16,2,128,128]{3,2,1,0:T(8,128)(2,1)S(1)} %get-tuple-element.32), channel_id=1, replica_groups={{0,16,32,48,64,80,96,112,128,144,160,176,192,208,224,240},{8,24,40,56,7..., dimensions={0} | all-to-all | bytes 2097152 | tf_op jit(solution)/shard_map/all_to_all | solution.py:198
  180.7 1.6 shard_map.83
  182.3 14.8 %all_to_all.89.terms = bf16[8,2,128,128]{3,2,1,0:T(8,128)(2,1)S(1)} all-to-all(bf16[8,2,128,128]{3,2,1,0:T(8,128)(2,1)S(1)} %shard_map.83), channel_id=1, replica_groups=mesh['prow'=32,'pcol'=8] {'pcol'}, dimensions={0} | all-to-all | bytes 1048576 | tf_op jit(solution)/shard_map/all_to_all | solution.py:202
  197.5 14.6 %all_to_all.90 = bf16[16,2,128,128]{3,2,1,0:T(8,128)(2,1)S(1)} all-to-all(bf16[16,2,128,128]{3,2,1,0:T(8,128)(2,1)S(1)} %get-tuple-element.34), channel_id=1, replica_groups={{0,16,32,48,64,80,96,112,128,144,160,176,192,208,224,240},{8,24,40,56,7..., dimensions={0} | all-to-all | bytes 2097152 | tf_op jit(solution)/shard_map/all_to_all | solution.py:198
  212.3 1.6 shard_map.85
  213.9 14.5 %all_to_all.91.terms = bf16[8,2,128,128]{3,2,1,0:T(8,128)(2,1)S(1)} all-to-all(bf16[8,2,128,128]{3,2,1,0:T(8,128)(2,1)S(1)} %shard_map.85), channel_id=1, replica_groups=mesh['prow'=32,'pcol'=8] {'pcol'}, dimensions={0} | all-to-all | bytes 1048576 | tf_op jit(solution)/shard_map/all_to_all | solution.py:202
  228.7 14.5 %all_to_all.92 = bf16[16,2,128,128]{3,2,1,0:T(8,128)(2,1)S(1)} all-to-all(bf16[16,2,128,128]{3,2,1,0:T(8,128)(2,1)S(1)} %get-tuple-element.36), channel_id=1, replica_groups={{0,16,32,48,64,80,96,112,128,144,160,176,192,208,224,240},{8,24,40,56,7..., dimensions={0} | all-to-all | bytes 2097152 | tf_op jit(solution)/shard_map/all_to_all | solution.py:198
  245.1 14.5 %all_to_all.93.terms = bf16[8,2,128,128]{3,2,1,0:T(8,128)(2,1)S(1)} all-to-all(bf16[8,2,128,128]{3,2,1,0:T(8,128)(2,1)S(1)} %shard_map.87), channel_id=1, replica_groups=mesh['prow'=32,'pcol'=8] {'pcol'}, dimensions={0} | all-to-all | bytes 1048576 | tf_op jit(solution)/shard_map/all_to_all | solution.py:202
  260.0 14.4 %all_to_all.94 = bf16[16,2,128,128]{3,2,1,0:T(8,128)(2,1)S(1)} all-to-all(bf16[16,2,128,128]{3,2,1,0:T(8,128)(2,1)S(1)} %get-tuple-element.38), channel_id=1, replica_groups={{0,16,32,48,64,80,96,112,128,144,160,176,192,208,224,240},{8,24,40,56,7..., dimensions={0} | all-to-all | bytes 2097152 | tf_op jit(solution)/shard_map/all_to_all | solution.py:198
  275.0 1.6 shard_map.89
  276.5 16.1 %all_to_all.95.terms = bf16[8,2,128,128]{3,2,1,0:T(8,128)(2,1)S(1)} all-to-all(bf16[8,2,128,128]{3,2,1,0:T(8,128)(2,1)S(1)} %shard_map.89), channel_id=1, replica_groups=mesh['prow'=32,'pcol'=8] {'pcol'}, dimensions={0} | all-to-all | bytes 1048576 | tf_op jit(solution)/shard_map/all_to_all | solution.py:202
  (55 shorter events, 15.8 us)
Async XLA Ops:
  0.0 5.0 %copy-start.1 = (s32[4,8,6]{1,0,2:T(4,128)S(1)}, s32[4,8,6]{1,0,2:T(4,128)}, u32[]{:S(2)}) copy-start(s32[4,8,6]{1,0,2:T(4,128)} %param.11) | copy-start | bytes 2308
  0.0 5.1 %copy-start = (s32[4,8,6]{1,0,2:T(4,128)S(1)}, s32[4,8,6]{1,0,2:T(4,128)}, u32[]{:S(2)}) copy-start(s32[4,8,6]{1,0,2:T(4,128)} %param.13) | copy-start | bytes 2308
  1.7 5.2 %collective-permute-start.2 = (bf16[16,128,128]{2,1,0:T(8,128)(2,1)S(1)}, bf16[16,128,128]{2,1,0:T(8,128)(2,1)S(1)}, u32[]{:S(2)}, u32[]{:S(2)}) collective-permute-start(bf16[16,128,128]{2,1,0:T(8,128)(2,1)S(1)} %get-tuple-element.24), channel_id=1, source_target_pairs={{0,8},{8,0},{16,24},{24,16},{32,40},{40,32},{48,56},{56,48},{64,72... | collective-permute-start | bytes 1572872 | tf_op jit(solution)/shard_map/ppermute | solution.py:179
  5.0 1.6 collective-permute-start
  5.1 1.5 collective-permute-start.1
  6.9 44.0 %collective-permute-start.4 = (bf16[4,8,6,128,128]{4,3,2,1,0:T(8,128)(2,1)}, bf16[4,8,6,128,128]{4,3,2,1,0:T(8,128)(2,1)S(1)}, u32[]{:S(2)}, u32[]{:S(2)}) collective-permute-start(bf16[4,8,6,128,128]{4,3,2,1,0:T(8,128)(2,1)} %own.9), channel_id=1, source_target_pairs={{0,8},{8,0},{16,24},{24,16},{32,40},{40,32},{48,56},{56,48},{64,72... | collective-permute-start | bytes 18874376 | tf_op jit(solution)/shard_map/ppermute | solution.py:179
  7.4 79.3 %collective-permute-start.3 = (bf16[4,8,6,128,128]{4,3,2,1,0:T(8,128)(2,1)}, bf16[4,8,6,128,128]{4,3,2,1,0:T(8,128)(2,1)S(1)}, u32[]{:S(2)}, u32[]{:S(2)}) collective-permute-start(bf16[4,8,6,128,128]{4,3,2,1,0:T(8,128)(2,1)} %own.13), channel_id=1, source_target_pairs={{0,8},{8,0},{16,24},{24,16},{32,40},{40,32},{48,56},{56,48},{64,72... | collective-permute-start | bytes 18874376 | tf_op jit(solution)/shard_map/ppermute | solution.py:179
  7.5 24.6 %collective-permute-start.5 = (bf16[18,128,128]{2,1,0:T(8,128)(2,1)S(1)}, bf16[18,128,128]{2,1,0:T(8,128)(2,1)S(1)}, u32[]{:S(2)}, u32[]{:S(2)}) collective-permute-start(bf16[18,128,128]{2,1,0:T(8,128)(2,1)S(1)} %get-tuple-element.27.mine), channel_id=1, source_target_pairs={{8,11},{9,12},{10,13},{11,14},{12,15},{13,8},{14,9},{15,10},{24,27... | collective-permute-start | bytes 1769480 | tf_op jit(solution)/shard_map/ppermute | solution.py:195
  32.3 54.4 %slice-start.2 = ((s8[6291456]{0:T(1024)(128)(4,1)}), s8[4194304]{0:T(1024)(128)(4,1)S(1)}, s32[]{:S(2)}) async-start(s8[6291456]{0:T(1024)(128)(4,1)} %bitcast.41), calls=%async_computation.18 | async-start | bytes 8388608
  51.0 35.7 %slice-start.3 = ((s8[6291456]{0:T(1024)(128)(4,1)}), s8[2097152]{0:T(1024)(128)(4,1)S(1)}, s32[]{:S(2)}) async-start(s8[6291456]{0:T(1024)(128)(4,1)} %bitcast.41), calls=%async_computation.19 | async-start | bytes 4194304
  148.9 31.9 %slice-start = ((s8[6291456]{0:T(1024)(128)(4,1)}), s8[4194304]{0:T(1024)(128)(4,1)S(1)}, s32[]{:S(2)}) async-start(s8[6291456]{0:T(1024)(128)(4,1)} %bitcast.39), calls=%async_computation.16 | async-start | bytes 8388608
  149.4 31.3 %slice-start.1 = ((s8[6291456]{0:T(1024)(128)(4,1)}), s8[2097152]{0:T(1024)(128)(4,1)S(1)}, s32[]{:S(2)}) async-start(s8[6291456]{0:T(1024)(128)(4,1)} %bitcast.39), calls=%async_computation.17 | async-start | bytes 4194304
  292.9 1.5 collective-permute-start.6
